TPU v7x, 128 devices: a whole 4x4x4 slice. The times are simulated.
128 devices in a mesh: gx: 8 (over x, core), gy: 16 (over y, z).
Axes of the slice: x: 4, y: 4, z: 4, core: 2. Of those that a mesh axis runs over, the one named last changes fastest.
Arguments:
- values: float32 [32768, 128], P(('gx', 'gy')), may hold values from -6 to 6
- noise: float32 [32768, 128], P(('gx', 'gy')), may hold values from 0.1 to 1
- fractions: float32 [3, 32768, 128], P(None, ('gx', 'gy')), may hold values from 0 to 1
- cell_xy: int32 [2, 32768, 128], P(None, ('gx', 'gy')), may hold values from 0 to 7
- cell_z: int32 [32768, 128], P(('gx', 'gy')), may hold values from 0 to 255
- tile_grid: int32 [32768], P(('gx', 'gy')), may hold values from 0 to 31
- counts: int32 [32768], P(('gx', 'gy')), may hold values from 1 to 128, as said below
- rate_x: float32 [512], replicated, may hold values from 0.01 to 4
- rate_y: float32 [512], replicated, may hold values from 0.01 to 4
- rate_z: float32 [256], replicated, may hold values from 0.01 to 4
Outputs:
- product: float32 [32768, 128], P(('gx', 'gy'))
Inputs may be any that keep to these rules, and one draw needn't show every extreme that they name: `counts`: every fifth point tile, counted from tile 0, is full. `tile_grid`: A point tile's grid tile is numbered within its own device's block of the grid.
All inputs are finite; a program needn't handle non-finite values.
Results may differ from a plain program's by a relative error of at most 0.00005.
Values sent between devices are 32-bit elements; how exact they have to be, the bound alone decides.
No kernel may reach another device: no remote copies, remote signals or barrier semaphores. Data moves between devices by JAX's collectives and lax.ppermute only.
A program may use at most 128 MiB of HBM per device.

v0:
```python
import math

import jax
import jax.numpy as jnp
from jax import lax
from jax.sharding import PartitionSpec as P

TILE = 8


PRECISE = lax.Precision.HIGHEST


def extended(block, sides, width):
    for axis, dim in sides:
        count = lax.axis_size(axis)
        forward = [(i, i + 1) for i in range(count - 1)]
        forward.append((count - 1, 0))
        backward = [(target, source) for source, target in forward]
        low = lax.ppermute(
            lax.slice_in_dim(block, block.shape[dim] - width, None, axis=dim), axis, forward
        )
        high = lax.ppermute(lax.slice_in_dim(block, 0, width, axis=dim), axis, backward)
        block = jnp.concatenate([low, block, high], axis=dim)
    return block


def cubic_taps(fraction):
    square = fraction * fraction
    cubed = square * fraction
    return (
        -0.5 * cubed + square - 0.5 * fraction,
        1.5 * cubed - 2.5 * square + 1.0,
        -1.5 * cubed + 2.0 * square + 0.5 * fraction,
        0.5 * cubed - 0.5 * square,
    )


def cas_table(length):
    counter = jnp.arange(length, dtype=jnp.int32)
    phase_mod = counter[:, None] * counter[None, :] % length
    radians = phase_mod.astype(jnp.float32) * (2.0 * math.pi / length)
    return jnp.cos(radians) + jnp.sin(radians)


def dense_weights(taps, start, length, periodic):
    box_span = jnp.arange(length, dtype=jnp.int32)
    weight_sum = jnp.zeros(start.shape + (length,), jnp.float32)
    for offset in range(4):
        position = start + offset
        if periodic:
            position = position % length
        weight_sum = weight_sum + jnp.where(
            position[..., None] == box_span, taps[offset][..., None], 0.0
        )
    return weight_sum


def body(values, noise, fractions, cell_xy, cell_z, tile_grid, counts, rate_x, rate_y, rate_z):
    tile_count, point_count = values.shape
    ranks_x = lax.axis_size("gx")
    ranks_y = lax.axis_size("gy")
    full_x = rate_x.shape[0]
    full_y = rate_y.shape[0]
    depth = rate_z.shape[0]
    cells_x = full_x // ranks_x
    cells_y = full_y // ranks_y
    rows_x = cells_x // TILE
    rows_y = cells_y // TILE
    grid_tiles = rows_x * rows_y
    box_side = TILE + 4
    tile_block = math.gcd(tile_count, 64)
    block_count = tile_count // tile_block
    is_live = jnp.arange(point_count, dtype=jnp.int32)[None, :] < counts[:, None]
    source = jnp.where(is_live, values, 0.0)
    catalog = jnp.arange(grid_tiles, dtype=jnp.int32)

    def blocked(array):
        return array.reshape((block_count, tile_block) + array.shape[1:])

    tile_items = (
        blocked(fractions[0]),
        blocked(fractions[1]),
        blocked(fractions[2]),
        blocked(cell_xy[0]),
        blocked(cell_xy[1]),
        blocked(cell_z),
        blocked(tile_grid),
        blocked(source),
    )

    def tile_weights(tile_item):
        frac_x, frac_y, frac_z, start_x, start_y, start_z, owner_tile, block_source = tile_item
        wide_x = dense_weights(cubic_taps(frac_x), start_x + 1, box_side, False)
        wide_y = dense_weights(cubic_taps(frac_y), start_y + 1, box_side, False)
        plane_weight = (wide_x[..., :, None] * wide_y[..., None, :]).reshape(
            frac_x.shape + (box_side * box_side,)
        )
        column_weight = dense_weights(cubic_taps(frac_z), start_z - 1, depth, True)
        selector = (owner_tile[:, None] == catalog[None, :]).astype(jnp.float32)
        return (plane_weight, column_weight, selector, block_source)

    def spread_step(accum, tile_item):
        plane_weight, column_weight, selector, block_source = tile_weights(tile_item)
        tile_boxes = jnp.einsum(
            "bpq,bpz->bqz", plane_weight, column_weight * block_source[..., None], precision=PRECISE
        )
        return (accum + jnp.einsum("bg,bqz->gqz", selector, tile_boxes, precision=PRECISE), None)

    accum_start = jnp.zeros((grid_tiles, box_side * box_side, depth), jnp.float32)
    accum, _ = lax.scan(spread_step, accum_start, tile_items)
    cubes = accum.reshape(rows_x, rows_y, box_side, box_side, depth).transpose(0, 2, 1, 3, 4)
    leading = cubes[:, :TILE].reshape(cells_x, rows_y, box_side, depth)
    trailing = jnp.pad(cubes[:, TILE:], ((0, 0), (0, TILE - 4), (0, 0), (0, 0), (0, 0))).reshape(
        cells_x, rows_y, box_side, depth
    )
    strips = (
        jnp.pad(leading, ((0, 4), (0, 0), (0, 0), (0, 0)))
        + jnp.pad(trailing, ((TILE, 0), (0, 0), (0, 0), (0, 0)))[: cells_x + 4]
    )
    leading = strips[:, :, :TILE].reshape(cells_x + 4, cells_y, depth)
    trailing = jnp.pad(strips[:, :, TILE:], ((0, 0), (0, 0), (0, TILE - 4), (0, 0))).reshape(
        cells_x + 4, cells_y, depth
    )
    padded = (
        jnp.pad(leading, ((0, 0), (0, 4), (0, 0)))
        + jnp.pad(trailing, ((0, 0), (TILE, 0), (0, 0)))[:, : cells_y + 4]
    )
    widened = extended(padded, (("gx", 0), ("gy", 1)), 2)
    folded = jnp.concatenate(
        [
            widened[4:6] + widened[0:2],
            widened[6 : cells_x + 2],
            widened[cells_x + 2 : cells_x + 4] + widened[cells_x + 6 : cells_x + 8],
        ],
        0,
    )
    spread_grid = jnp.concatenate(
        [
            folded[:, 4:6] + folded[:, 0:2],
            folded[:, 6 : cells_y + 2],
            folded[:, cells_y + 2 : cells_y + 4] + folded[:, cells_y + 6 : cells_y + 8],
        ],
        1,
    )
    table_x = cas_table(full_x)
    table_y = cas_table(full_y)
    table_z = cas_table(depth)
    planes_dev = depth // (ranks_x * ranks_y)
    turned = jnp.einsum("xyz,zk->xky", spread_grid, table_z, precision=PRECISE)
    pencils = lax.all_to_all(turned, "gy", split_axis=1, concat_axis=2, tiled=True)
    pencils = jnp.einsum("xzy,yk->xzk", pencils, table_y, precision=PRECISE)
    planes = lax.all_to_all(pencils, "gx", split_axis=1, concat_axis=0, tiled=True)
    z_start = lax.axis_index("gy") * (depth // ranks_y) + lax.axis_index("gx") * planes_dev
    planes = jnp.einsum("xzy,xk->kzy", planes, table_x, precision=PRECISE)
    local_rate = lax.dynamic_slice_in_dim(rate_z, z_start, planes_dev)
    denom = 1.0 + rate_x[:, None, None] + rate_y[None, None, :] + local_rate[None, :, None]
    weighted = planes * (4.0 / (denom * denom))
    inverse = jnp.einsum("kzy,kx->xzy", weighted, table_x, precision=PRECISE)
    slabs = lax.all_to_all(inverse, "gx", split_axis=0, concat_axis=1, tiled=True)
    slabs = jnp.einsum("xzy,yk->xzk", slabs, table_y, precision=PRECISE)
    returned = lax.all_to_all(slabs, "gy", split_axis=2, concat_axis=1, tiled=True)
    grid_field = jnp.einsum("xzy,zk->xyk", returned, table_z, precision=PRECISE)
    grid_field = grid_field / (full_x * full_y * depth)
    bordered = extended(grid_field, (("gx", 0), ("gy", 1)), 2)
    leading = bordered[:cells_x].reshape(rows_x, TILE, cells_y + 4, depth)
    trailing = jnp.pad(bordered[TILE:], ((0, 4), (0, 0), (0, 0))).reshape(
        rows_x, TILE, cells_y + 4, depth
    )[:, :4]
    strips = jnp.concatenate([leading, trailing], 1)
    leading = strips[:, :, :cells_y].reshape(rows_x, box_side, rows_y, TILE, depth)
    trailing = jnp.pad(strips[:, :, TILE:], ((0, 0), (0, 0), (0, 4), (0, 0))).reshape(
        rows_x, box_side, rows_y, TILE, depth
    )[:, :, :, :4]
    grid_boxes = (
        jnp.concatenate([leading, trailing], 3)
        .transpose(0, 2, 1, 3, 4)
        .reshape(grid_tiles, box_side * box_side, depth)
    )

    def sample_step(carry, tile_item):
        plane_weight, column_weight, selector, block_source = tile_weights(tile_item)
        local_boxes = jnp.einsum("bg,gqz->bqz", selector, grid_boxes, precision=PRECISE)
        along_z = jnp.einsum("bpq,bqz->bpz", plane_weight, local_boxes, precision=PRECISE)
        return (carry, jnp.sum(along_z * column_weight, axis=-1))

    _, sampled = lax.scan(sample_step, None, tile_items)
    sampled = sampled.reshape(tile_count, point_count)
    return jnp.where(is_live, noise * values + sampled, 0.0)


def solution(mesh):
    in_specs = (
        P(("gx", "gy"), None),
        P(("gx", "gy"), None),
        P(None, ("gx", "gy"), None),
        P(None, ("gx", "gy"), None),
        P(("gx", "gy"), None),
        P(("gx", "gy")),
        P(("gx", "gy")),
        P(),
        P(),
        P(),
    )
    out_specs = P(("gx", "gy"), None)
    return jax.shard_map(body, mesh=mesh, in_specs=in_specs, out_specs=out_specs, check_vma=False)
```

profile of v0, /device:TPU:1, one launch (start us, length us, event | category | flops | bytes accessed | tf_op | source)
XLA Modules:
  0.0 639.8 jit_solution(8219770264727767321)
XLA Ops:
  3.8 176.4 %while.33 = (s32[]{:T(128)}, f32[32,144,256]{2,0,1:T(8,128)}, s32[4,64]{1,0:T(4,128)S(1)}, s32[4,64,128]{2,1,0:T(8,128)S(1)}, f32[4,64,128]{2,1,0:T(8,128)S(1)},...) while((s32[]{:T(128)}, f32[32,144,256]{2,0,1:T(8,128)}, ...), condition=%wide.region_1.2_spmd.clone, body=%wide.region_0.1_spmd.clone.sunk | while | flops 4561586176 | bytes 41190292 | solution.py:111
  5.7 26.4 %fusion.201 = f32[64,144,256]{2,1,0:T(8,128)} fusion(f32[64,128,144]{1,0,2:T(8,128)S(1)} %bitcast.308, f32[64,128]{1,0:T(8,128)S(1)} %dynamic-slice_bitcast_fusion.2, f32[64,128]{1,0:T(8,128)S(1)} %get-tuple-element.943, s32[64,128]{1,0:T(8,128)S(1)} %get-tuple-element.944, f32[64,128]{1,0:T(8,128)S(1)} %get-tuple-element.945, ...), kind=kOutput, calls=%fused_computation.93.clone.2 | convolution fusion | flops 3649044480 | bytes 14450688 | tf_op jit(solution)/shard_map/while/body/eval_jaxpr/bpq,bpz->bqz/dot_general | solution.py:105
  32.1 14.8 %select_add_fusion.14 = f32[32,144,256]{2,0,1:T(8,128)} fusion(f32[32,144,256]{2,0,1:T(8,128)} %get-tuple-element.964, pred[]{:T(512)S(6)} %compare.58, f32[64,144,256]{2,1,0:T(8,128)} %fusion.201, s32[64]{0:T(128)S(1)} %fusion.202), kind=kOutput, calls=%fused_computation.107.clone.1 | convolution fusion | flops 908331008 | bytes 18874624 | tf_op jit(solution)/shard_map/while/body/eval_jaxpr/bg,bqz->gqz/dot_general | solution.py:108
  48.8 26.4 %fusion.201 = f32[64,144,256]{2,1,0:T(8,128)} fusion(f32[64,128,144]{1,0,2:T(8,128)S(1)} %bitcast.308, f32[64,128]{1,0:T(8,128)S(1)} %dynamic-slice_bitcast_fusion.2, f32[64,128]{1,0:T(8,128)S(1)} %get-tuple-element.943, s32[64,128]{1,0:T(8,128)S(1)} %get-tuple-element.944, f32[64,128]{1,0:T(8,128)S(1)} %get-tuple-element.945, ...), kind=kOutput, calls=%fused_computation.93.clone.2 | convolution fusion | flops 3649044480 | bytes 14450688 | tf_op jit(solution)/shard_map/while/body/eval_jaxpr/bpq,bpz->bqz/dot_general | solution.py:105
  75.2 16.1 %select_add_fusion.14 = f32[32,144,256]{2,0,1:T(8,128)} fusion(f32[32,144,256]{2,0,1:T(8,128)} %get-tuple-element.964, pred[]{:T(512)S(6)} %compare.58, f32[64,144,256]{2,1,0:T(8,128)} %fusion.201, s32[64]{0:T(128)S(1)} %fusion.202), kind=kOutput, calls=%fused_computation.107.clone.1 | convolution fusion | flops 908331008 | bytes 18874624 | tf_op jit(solution)/shard_map/while/body/eval_jaxpr/bg,bqz->gqz/dot_general | solution.py:108
  93.2 26.4 %fusion.201 = f32[64,144,256]{2,1,0:T(8,128)} fusion(f32[64,128,144]{1,0,2:T(8,128)S(1)} %bitcast.308, f32[64,128]{1,0:T(8,128)S(1)} %dynamic-slice_bitcast_fusion.2, f32[64,128]{1,0:T(8,128)S(1)} %get-tuple-element.943, s32[64,128]{1,0:T(8,128)S(1)} %get-tuple-element.944, f32[64,128]{1,0:T(8,128)S(1)} %get-tuple-element.945, ...), kind=kOutput, calls=%fused_computation.93.clone.2 | convolution fusion | flops 3649044480 | bytes 14450688 | tf_op jit(solution)/shard_map/while/body/eval_jaxpr/bpq,bpz->bqz/dot_general | solution.py:105
  119.6 16.1 %select_add_fusion.14 = f32[32,144,256]{2,0,1:T(8,128)} fusion(f32[32,144,256]{2,0,1:T(8,128)} %get-tuple-element.964, pred[]{:T(512)S(6)} %compare.58, f32[64,144,256]{2,1,0:T(8,128)} %fusion.201, s32[64]{0:T(128)S(1)} %fusion.202), kind=kOutput, calls=%fused_computation.107.clone.1 | convolution fusion | flops 908331008 | bytes 18874624 | tf_op jit(solution)/shard_map/while/body/eval_jaxpr/bg,bqz->gqz/dot_general | solution.py:108
  137.7 26.4 %fusion.201 = f32[64,144,256]{2,1,0:T(8,128)} fusion(f32[64,128,144]{1,0,2:T(8,128)S(1)} %bitcast.308, f32[64,128]{1,0:T(8,128)S(1)} %dynamic-slice_bitcast_fusion.2, f32[64,128]{1,0:T(8,128)S(1)} %get-tuple-element.943, s32[64,128]{1,0:T(8,128)S(1)} %get-tuple-element.944, f32[64,128]{1,0:T(8,128)S(1)} %get-tuple-element.945, ...), kind=kOutput, calls=%fused_computation.93.clone.2 | convolution fusion | flops 3649044480 | bytes 14450688 | tf_op jit(solution)/shard_map/while/body/eval_jaxpr/bpq,bpz->bqz/dot_general | solution.py:105
  164.1 16.1 %select_add_fusion.14 = f32[32,144,256]{2,0,1:T(8,128)} fusion(f32[32,144,256]{2,0,1:T(8,128)} %get-tuple-element.964, pred[]{:T(512)S(6)} %compare.58, f32[64,144,256]{2,1,0:T(8,128)} %fusion.201, s32[64]{0:T(128)S(1)} %fusion.202), kind=kOutput, calls=%fused_computation.107.clone.1 | convolution fusion | flops 908331008 | bytes 18874624 | tf_op jit(solution)/shard_map/while/body/eval_jaxpr/bg,bqz->gqz/dot_general | solution.py:108
  180.2 6.5 %reshape.918 = f32[8,4,12,12,256]{4,1,0,3,2:T(4,128)} reshape(f32[32,144,256]{2,0,1:T(8,128)} %get-tuple-element.541) | data formatting | bytes 9437184 | tf_op jit(solution)/shard_map/reshape | solution.py:112
  186.7 1.9 slice.141
  188.6 2.6 slice.140
  192.2 2.2 pad_bitcast_fusion
  195.8 2.6 collective-permute-start
  198.4 1.4 collective-permute-done
  199.8 2.4 collective-permute-done.1
  202.2 1.7 collective-permute-start.2
  203.9 4.7 collective-permute-start.3
  208.6 4.0 collective-permute-done.2
  214.2 2.9 fusion.104
  217.1 4.9 copy.94
  222.0 4.5 reshape.935
  226.5 32.7 %all_to_all.72 = f32[16,1,32768]{2,1,0:T(1,128)} all-to-all(f32[16,1,32768]{2,1,0:T(1,128)S(1)} %reshape.935), channel_id=1, replica_groups=mesh['gx'=8,'gy'=16] {'gy'}, dimensions={0} | all-to-all | bytes 4194304 | tf_op jit(solution)/shard_map/all_to_all | solution.py:151
  259.7 7.3 %reduce = f32[16,32768]{1,0:T(8,128)S(1)} reduce(f32[16,1,32768]{2,1,0:T(1,128)} %all_to_all.72, f32[]{:T(128)} %broadcast.1863), dimensions={1}, to_apply=%all_to_all.52.reduce_sub_computation | reduce | bytes 4194308 | tf_op jit(solution)/shard_map/all_to_all | solution.py:151
  267.0 3.0 reshape.936
  270.0 2.8 copy.95
  272.9 18.3 %fusion.112 = f32[64,16,512]{2,0,1:T(8,128)} fusion(f32[64,16,512]{0,2,1:T(8,128)S(1)} %bitcast.315), kind=kOutput, calls=%fused_computation.237 | convolution fusion | flops 3225157632 | bytes 4194304 | tf_op jit(solution)/shard_map/xzy,yk->xzk/dot_general | solution.py:152
  291.2 6.8 %all-to-all-start.1 = ((f32[64,16,512]{2,0,1:T(8,128)}), f32[64,16,512]{2,0,1:T(8,128)S(1)}, u32[]{:S(2)}, u32[]{:S(2)}) async-start(f32[64,16,512]{2,0,1:T(8,128)} %fusion.112), calls=%async_computation.1 | async-start | bytes 4194304 | tf_op jit(solution)/shard_map/all_to_all | solution.py:153
  299.2 24.9 %all-to-all-done.1 = f32[64,16,512]{2,0,1:T(8,128)S(1)} async-done(((f32[64,16,512]{2,0,1:T(8,128)}), f32[64,16,512]{2,0,1:T(8,128)S(1)}, u32[]{:S(2)}, u32[]{:S(2)}) %all-to-all-start.1) | async-done | bytes 2097184 | tf_op jit(solution)/shard_map/all_to_all | solution.py:153
  324.3 7.6 %fusion.114 = f32[512,2,512]{2,0,1:T(8,128)S(1)} fusion(f32[512,2,512]{2,0,1:T(8,128)S(1)} %bitcast.324), kind=kOutput, calls=%fused_computation.239 | convolution fusion | flops 3225157632 | bytes 4194304 | tf_op jit(solution)/shard_map/xzy,xk->kzy/dot_general | solution.py:155
  331.9 8.4 %fusion.99 = f32[512,2,512]{2,0,1:T(8,128)S(1)} fusion(f32[512,2,512]{2,0,1:T(8,128)S(1)} %fusion.114, f32[2]{0:T(128)S(1)} %dynamic_slice.156, f32[512,512]{1,0:T(8,128)S(1)} %copy-done.2), kind=kOutput, calls=%fused_computation.222 | convolution fusion | flops 3227254784 | bytes 5242888 | tf_op jit(solution)/shard_map/kzy,kx->xzy/dot_general | solution.py:159
  340.4 1.6 copy.101
  342.0 29.8 %all_to_all.73 = f32[512,2,512]{2,1,0:T(2,128)S(1)} all-to-all(f32[512,2,512]{2,1,0:T(2,128)S(1)} %copy.101), channel_id=1, replica_groups=mesh['gx'=8,'gy'=16] {'gx'}, dimensions={0} | all-to-all | bytes 4194304 | tf_op jit(solution)/shard_map/all_to_all | solution.py:160
  373.0 2.4 all_to_all.63
  375.4 10.3 %fusion.110 = f32[64,16,512]{2,1,0:T(8,128)S(1)} fusion(f32[64,16,512]{2,1,0:T(8,128)} %all_to_all.63), kind=kOutput, calls=%fused_computation.235 | convolution fusion | flops 3225157632 | bytes 4194304 | tf_op jit(solution)/shard_map/xzy,yk->xzk/dot_general | solution.py:161
  385.7 4.2 copy.103
  389.9 4.5 reshape.937
  394.5 30.6 %all_to_all.74 = f32[16,1,32768]{2,1,0:T(1,128)} all-to-all(f32[16,1,32768]{2,1,0:T(1,128)S(1)} %reshape.937), channel_id=1, replica_groups=mesh['gx'=8,'gy'=16] {'gy'}, dimensions={0} | all-to-all | bytes 4194304 | tf_op jit(solution)/shard_map/all_to_all | solution.py:162
  425.1 7.3 %reduce.1 = f32[16,32768]{1,0:T(8,128)S(1)} reduce(f32[16,1,32768]{2,1,0:T(1,128)} %all_to_all.74, f32[]{:T(128)} %broadcast.1863), dimensions={1}, to_apply=%all_to_all.64.reduce_sub_computation | reduce | bytes 4194308 | tf_op jit(solution)/shard_map/all_to_all | solution.py:162
  432.4 3.1 reshape.938
  435.5 5.5 copy.105
  440.9 5.2 copy.106
  446.1 4.4 convolution_multiply_fusion
  450.6 2.4 collective-permute-start.4
  453.0 1.3 collective-permute-done.4
  454.3 2.7 collective-permute-done.5
  457.6 4.5 collective-permute-start.7
  462.1 3.0 collective-permute-done.6
  465.7 1.3 copy-done.1
  467.4 1.6 slice-done
  470.7 5.2 copy.107
  475.9 6.4 %reshape.927 = f32[32,144,256]{2,0,1:T(8,128)} reshape(f32[8,4,12,12,256]{4,1,0,3,2:T(4,128)} %copy.107) | data formatting | bytes 9437184 | tf_op jit(solution)/shard_map/reshape | solution.py:178
  482.4 156.3 %while.32 = (s32[]{:T(128)}, f32[4,64,128]{2,1,0:T(8,128)S(1)}, s32[4,64,128]{2,1,0:T(8,128)S(1)}, f32[4,64,128]{2,1,0:T(8,128)S(1)}, s32[4,64,128]{2,1,0:T(8,12...) while((s32[]{:T(128)}, f32[4,64,128]{2,1,0:T(8,128)S(1)}, ...), condition=%wide.region_4.5_spmd.clone, body=%wide.region_2.4_spmd.clone.sunk | while | flops 4561315840 | bytes 55346080 | solution.py:187
  483.4 1.2 add_select_fusion.12
  485.0 4.0 fusion.193
  488.9 32.5 %multiply_reduce_fusion.2 = f32[64,128]{1,0:T(8,128)S(1)} fusion(f32[64,128]{1,0:T(8,128)S(1)} %get-tuple-element.893, s32[64,128]{1,0:T(8,128)S(1)} %get-tuple-element.894, f32[64,128]{1,0:T(8,128)S(1)} %get-tuple-element.895, s32[64,128]{1,0:T(8,128)S(1)} %get-tuple-element.896, f32[64,128]{1,0:T(8,128)S(1)} %get-tuple-element.897, ...), kind=kOutput, calls=%fused_computation.4.clone.1 | convolution fusion | flops 3651133440 | bytes 14450688 | tf_op jit(solution)/shard_map/while/body/eval_jaxpr/bpq,bqz->bpz/dot_general | solution.py:184
  522.5 1.2 add_select_fusion.12
  524.0 3.9 fusion.193
  528.0 32.5 %multiply_reduce_fusion.2 = f32[64,128]{1,0:T(8,128)S(1)} fusion(f32[64,128]{1,0:T(8,128)S(1)} %get-tuple-element.893, s32[64,128]{1,0:T(8,128)S(1)} %get-tuple-element.894, f32[64,128]{1,0:T(8,128)S(1)} %get-tuple-element.895, s32[64,128]{1,0:T(8,128)S(1)} %get-tuple-element.896, f32[64,128]{1,0:T(8,128)S(1)} %get-tuple-element.897, ...), kind=kOutput, calls=%fused_computation.4.clone.1 | convolution fusion | flops 3651133440 | bytes 14450688 | tf_op jit(solution)/shard_map/while/body/eval_jaxpr/bpq,bqz->bpz/dot_general | solution.py:184
  561.5 1.2 add_select_fusion.12
  563.1 4.0 fusion.193
  567.1 32.5 %multiply_reduce_fusion.2 = f32[64,128]{1,0:T(8,128)S(1)} fusion(f32[64,128]{1,0:T(8,128)S(1)} %get-tuple-element.893, s32[64,128]{1,0:T(8,128)S(1)} %get-tuple-element.894, f32[64,128]{1,0:T(8,128)S(1)} %get-tuple-element.895, s32[64,128]{1,0:T(8,128)S(1)} %get-tuple-element.896, f32[64,128]{1,0:T(8,128)S(1)} %get-tuple-element.897, ...), kind=kOutput, calls=%fused_computation.4.clone.1 | convolution fusion | flops 3651133440 | bytes 14450688 | tf_op jit(solution)/shard_map/while/body/eval_jaxpr/bpq,bqz->bpz/dot_general | solution.py:184
  602.2 3.9 fusion.193
  606.1 32.5 %multiply_reduce_fusion.2 = f32[64,128]{1,0:T(8,128)S(1)} fusion(f32[64,128]{1,0:T(8,128)S(1)} %get-tuple-element.893, s32[64,128]{1,0:T(8,128)S(1)} %get-tuple-element.894, f32[64,128]{1,0:T(8,128)S(1)} %get-tuple-element.895, s32[64,128]{1,0:T(8,128)S(1)} %get-tuple-element.896, f32[64,128]{1,0:T(8,128)S(1)} %get-tuple-element.897, ...), kind=kOutput, calls=%fused_computation.4.clone.1 | convolution fusion | flops 3651133440 | bytes 14450688 | tf_op jit(solution)/shard_map/while/body/eval_jaxpr/bpq,bqz->bpz/dot_general | solution.py:184
  (137 shorter events, 28.8 us)
Async XLA Ops:
  195.8 4.0 collective-permute-start
  198.4 3.8 collective-permute-start.1
  202.2 10.4 %collective-permute-start.2 = (f32[72,2,256]{2,0,1:T(8,128)S(1)}, f32[72,2,256]{2,0,1:T(8,128)S(1)}, u32[]{:S(2)}, u32[]{:S(2)}) collective-permute-start(f32[72,2,256]{2,0,1:T(8,128)S(1)} %get-tuple-element.716), channel_id=1, source_target_pairs={{0,1},{1,2},{2,3},{3,4},{4,5},{5,6},{6,7},{7,8},{8,9},{9,10},{10,1... | collective-permute-start | bytes 442376 | tf_op jit(solution)/shard_map/ppermute | solution.py:20
  203.9 8.7 %collective-permute-start.3 = (f32[72,2,256]{2,0,1:T(8,128)S(1)}, f32[72,2,256]{2,0,1:T(8,128)S(1)}, u32[]{:S(2)}, u32[]{:S(2)}) collective-permute-start(f32[72,2,256]{2,0,1:T(8,128)S(1)} %get-tuple-element.717), channel_id=1, source_target_pairs={{1,0},{2,1},{3,2},{4,3},{5,4},{6,5},{7,6},{8,7},{9,8},{10,9},{11,1... | collective-permute-start | bytes 442376 | tf_op jit(solution)/shard_map/ppermute | solution.py:23
  291.1 6.8 %copy-start.9 = (f32[256]{0:T(256)S(1)}, f32[256]{0:T(256)}, u32[]{:S(2)}) copy-start(f32[256]{0:T(256)} %param.23) | copy-start | bytes 3076
  291.1 6.9 %copy-start.8 = (f32[512]{0:T(512)S(1)}, f32[512]{0:T(512)}, u32[]{:S(2)}) copy-start(f32[512]{0:T(512)} %param.21) | copy-start | bytes 6148
  291.2 6.9 %copy-start.7 = (f32[512]{0:T(512)S(1)}, f32[512]{0:T(512)}, u32[]{:S(2)}) copy-start(f32[512]{0:T(512)} %param.22) | copy-start | bytes 6148
  291.2 32.9 %all-to-all-start.1 = ((f32[64,16,512]{2,0,1:T(8,128)}), f32[64,16,512]{2,0,1:T(8,128)S(1)}, u32[]{:S(2)}, u32[]{:S(2)}) async-start(f32[64,16,512]{2,0,1:T(8,128)} %fusion.112), calls=%async_computation.1 | async-start | bytes 4194304 | tf_op jit(solution)/shard_map/all_to_all | solution.py:153
  324.3 7.6 %copy-start.2 = (f32[512,512]{1,0:T(8,128)S(1)}, f32[512,512]{1,0:T(8,128)}, u32[]{:S(2)}) copy-start(f32[512,512]{1,0:T(8,128)} %broadcast_add_fusion) | copy-start | bytes 3145732
  450.6 3.7 collective-permute-start.4
  452.9 4.0 collective-permute-start.5
  457.0 8.1 %collective-permute-start.6 = (f32[68,2,256]{2,1,0:T(2,128)S(1)}, f32[68,2,256]{2,1,0:T(2,128)S(1)}, u32[]{:S(2)}, u32[]{:S(2)}) collective-permute-start(f32[68,2,256]{2,1,0:T(2,128)S(1)} %get-tuple-element.722), channel_id=1, source_target_pairs={{0,1},{1,2},{2,3},{3,4},{4,5},{5,6},{6,7},{7,8},{8,9},{9,10},{10,1... | collective-permute-start | bytes 417800 | tf_op jit(solution)/shard_map/ppermute | solution.py:20
  457.6 7.5 %collective-permute-start.7 = (f32[68,2,256]{2,1,0:T(2,128)S(1)}, f32[68,2,256]{2,1,0:T(2,128)S(1)}, u32[]{:S(2)}, u32[]{:S(2)}) collective-permute-start(f32[68,2,256]{2,1,0:T(2,128)S(1)} %get-tuple-element.723), channel_id=1, source_target_pairs={{1,0},{2,1},{3,2},{4,3},{5,4},{6,5},{7,6},{8,7},{9,8},{10,9},{11,1... | collective-permute-start | bytes 417800 | tf_op jit(solution)/shard_map/ppermute | solution.py:23
  465.5 1.5 copy-start.1
  467.2 1.7 slice-start
  475.9 6.4 %copy-start.5 = (f32[4,64,128]{2,1,0:T(8,128)S(1)}, f32[4,64,128]{2,1,0:T(8,128)}, u32[]{:S(2)}) copy-start(f32[4,64,128]{2,1,0:T(8,128)} %custom-call.1) | copy-start | bytes 393220
  482.3 156.3 %copy-start.3 = (f32[256,128]{1,0:T(8,128)S(1)}, f32[256,128]{1,0:T(8,128)}, u32[]{:S(2)}) copy-start(f32[256,128]{1,0:T(8,128)} %param.14) | copy-start | bytes 393220
  482.3 156.3 %copy-start.4 = (f32[256,128]{1,0:T(8,128)S(1)}, f32[256,128]{1,0:T(8,128)}, u32[]{:S(2)}) copy-start(f32[256,128]{1,0:T(8,128)} %param.15) | copy-start | bytes 393220
  482.3 156.3 %copy-start.6 = (s32[256]{0:T(256)S(1)}, s32[256]{0:T(256)}, u32[]{:S(2)}) copy-start(s32[256]{0:T(256)} %param.20) | copy-start | bytes 3076
  482.6 2.4 copy-start
  521.7 2.4 copy-start
  560.8 2.4 copy-start
  599.8 2.4 copy-start
where the time goes:
time: 649 us; the launch traced here: 640 us
  matrix products  366 us (56%)
  blocking collectives  93.1 us (14%)
  local copies, waits for them, and re-layouts  78.6 us (12%)
  waiting for transfers between devices  39.7 us (6%)
  other arithmetic  37.3 us (6%)
  starting transfers between devices  23.2 us (4%)
    dot_general x4, matrix products, sample_step(): jnp.einsum('bpq,bqz->bpz', plane_weight, local_boxes, precision=PRECISE)  130 us
    dot_general x4, matrix products, spread_step(): jnp.einsum('bpq,bpz->bqz', plane_weight, column_weight * block_source[......  106 us
    dot_general x4, matrix products, spread_step(): jnp.einsum('bg,bqz->gqz', selector, tile_boxes, precision=PRECISE)  63.2 us
    all_to_all x1, blocking collectives, body(): lax.all_to_all(turned, 'gy', split_axis=1, concat_axis=2, tiled=True)  32.7 us
    all_to_all x1, blocking collectives, body(): lax.all_to_all(slabs, 'gy', split_axis=2, concat_axis=1, tiled=True)  30.6 us
    all_to_all x1, blocking collectives, body(): lax.all_to_all(inverse, 'gx', split_axis=0, concat_axis=1, tiled=True)  29.8 us
    all_to_all x1, waiting for transfers between devices, body(): lax.all_to_all(pencils, 'gx', split_axis=1, concat_axis=0, tiled=True)  24.9 us
    dot_general x1, matrix products, body(): pencils = jnp.einsum('xzy,yk->xzk', pencils, table_y, precision=PRECISE)  18.3 us
  transfers between devices with their start and end apart: 9, of which 7 were waited for; matrix products, arithmetic and copies ran while one was open for 0% of the time, Pallas kernels for 0%

commit v1 on v0

v1 whole, which is shorter than its diff:
```python
import math

import jax
import jax.numpy as jnp
import ml_dtypes
import numpy as np
from jax import lax
from jax.experimental import pallas as pl
from jax.experimental.pallas import tpu as pltpu
from jax.sharding import PartitionSpec as P

NX, NY, NZ = 512, 512, 256
TILE = 8
PTS = 128
RX, RY = 8, 16
DEVS = RX * RY
BX, BY = NX // RX, NY // RY
GROW = BY // TILE
EY = BY + 3
SY, SX = 36, 72
BOX = 11
BLK = 40
HALO = ((0, -1), (65, 64), (66, 65))
CHUNK = 128

BF = jnp.bfloat16
F32 = jnp.float32
NN = (((1,), (0,)), ((), ()))
NT = (((1,), (1,)), ((), ()))


def halves(table):
    table = np.asarray(table, np.float32)
    high = table.astype(ml_dtypes.bfloat16)
    low = (table - high.astype(np.float32)).astype(ml_dtypes.bfloat16)
    return high, low


def cas(rows, columns, length):
    phase = np.outer(np.asarray(rows, np.int64), np.asarray(columns, np.int64)) % length
    angle = phase * (2.0 * math.pi / length)
    return np.cos(angle) + np.sin(angle)


def tables():
    cas_z = cas(np.arange(NZ), np.arange(NZ), NZ)
    cas_x = cas(np.arange(NX), np.arange(NX), NX)
    line = np.arange(EY) - 1
    full_y = cas(np.arange(NY), (np.arange(RY)[:, None] * BY + line[None, :]).reshape(-1) % NY, NY)
    full_y = full_y.reshape(NY, RY, EY)
    rows_y = np.zeros((NY, RY, BLK))
    rows_y[:, :, :EY] = full_y
    rows_y = rows_y.reshape(NY, RY * BLK)
    edge_y = np.zeros((NY, RY, 64))
    edge_y[:, :, :EY] = full_y
    edge_y = edge_y.reshape(NY, RY * 64)
    edge_x = cas(
        np.concatenate([np.arange(RX) * BX + offset for _, offset in HALO]) % NX, np.arange(NX), NX
    )
    edge_two = np.zeros((2, 48, NX))
    edge_two[0, :24] = edge_x
    edge_two[1, 24:] = edge_x
    return {
        "z": halves(cas_z),
        "x": halves(cas_x),
        "y": halves(rows_y),
        "yt": halves(rows_y.T),
        "ey": halves(edge_y),
        "ex2": halves(edge_two),
        "ex": halves(edge_x),
    }


def split(value):
    high = value.astype(BF)
    return high, (value - high.astype(F32)).astype(BF)


def mm(a, b, dims=NN):
    return lax.dot_general(a, b, dims, preferred_element_type=F32)


def mm3(a, b, dims=NN):
    return mm(a[0], b[0], dims) + (mm(a[0], b[1], dims) + mm(a[1], b[0], dims))


def cubic_taps(fraction):
    square = fraction * fraction
    cubed = square * fraction
    return (
        -0.5 * cubed + square - 0.5 * fraction,
        1.5 * cubed - 2.5 * square + 1.0,
        -1.5 * cubed + 2.0 * square + 0.5 * fraction,
        0.5 * cubed - 0.5 * square,
    )


def low_lanes(shape):
    return lax.broadcasted_iota(jnp.int32, shape, 1) < 64


def swap(a, b):
    low = low_lanes(a.shape)
    return (
        jnp.where(low, a, pltpu.roll(b, 64, 1)),
        jnp.where(low, pltpu.roll(a, 64, 1), b),
    )


def fill_taps(frac_ref, taps_ref):
    tiles = frac_ref.shape[1]

    def step(i, carry):
        rows = pl.ds(pl.multiple_of(i * 8, 8), 8)
        for axis in range(3):
            for offset, tap in enumerate(cubic_taps(frac_ref[axis, rows, :])):
                taps_ref[axis * 4 + offset, rows, :] = tap
        return carry

    lax.fori_loop(0, tiles // 8, step, 0)


def window(start, taps, length):
    delta = lax.broadcasted_iota(jnp.int32, (length, PTS), 0) - start
    weights = jnp.where(delta == 0, taps[0], 0.0)
    for offset in range(1, 4):
        weights = jnp.where(delta == offset, taps[offset], weights)
    return weights


def column(start, taps):
    delta = (lax.broadcasted_iota(jnp.int32, (NZ, PTS), 0) - (start - 1)) & (NZ - 1)
    weights = jnp.where(delta == 0, taps[0], 0.0)
    for offset in range(1, 4):
        weights = jnp.where(delta == offset, taps[offset], weights)
    return weights


def tile_rows(t, taps_ref, xy_ref, z_ref):
    row = pl.ds(t, 1)
    taps = [taps_ref[k, row, :] for k in range(12)]
    return taps, xy_ref[0, row, :], xy_ref[1, row, :], z_ref[row, :]


def spread_kernel(
    grid_ref, counts_ref, val_ref, frac_ref, xy_ref, z_ref, tzh_ref, tzl_ref, out_ref, taps_ref, pad_ref
):
    tiles = val_ref.shape[0]
    fill_taps(frac_ref, taps_ref)
    pad_ref[...] = jnp.zeros_like(pad_ref)
    slots = lax.broadcasted_iota(jnp.int32, (1, PTS), 1)

    def step(t, carry):
        taps, cell_x, cell_y, cell_z = tile_rows(t, taps_ref, xy_ref, z_ref)
        source = jnp.where(slots < counts_ref[t], val_ref[pl.ds(t, 1), :], 0.0)
        wide_x = window(cell_x, taps[0:4], 16)
        wide_y = window(cell_y, [tap * source for tap in taps[4:8]], 16)
        plane = jnp.concatenate([wide_y[q : q + 1] * wide_x for q in range(BOX)], 0)
        plane = split(plane)
        col = split(column(cell_z, taps[8:12]))
        box = mm3(plane, col, NT)
        g = grid_ref[t]
        gx = g // GROW
        gy = g - gx * GROW
        place = pl.ds(pl.multiple_of(gx * TILE, TILE), 16)
        for q in range(BOX):
            pad_ref[gy * TILE + q, place, :] += box[q * 16 : q * 16 + 16]
        return carry

    lax.fori_loop(0, tiles, step, 0)

    table = (tzh_ref[...], tzl_ref[...])

    def put(rows, first, second):
        turned = mm3(table, split(rows), NT)
        a, b = swap(turned[:DEVS], turned[DEVS:])
        out_ref[pl.ds(first, DEVS, stride=BLK), :] = a
        if second is not None:
            out_ref[pl.ds(second, DEVS, stride=BLK), :] = b

    for pair in range(SY // 2):
        y = 2 * pair
        rows = jnp.concatenate([pad_ref[y, 1:65, :], pad_ref[y + 1, 1:65, :]], 0)
        put(rows, y, y + 1 if y + 1 < EY else None)
    edges = [
        jnp.concatenate([pad_ref[:, at, :], jnp.zeros((64 - SY, NZ), F32)], 0) for at, _ in HALO
    ]
    put(jnp.concatenate([edges[0], edges[1]], 0), EY, EY + 1)
    put(jnp.concatenate([edges[2], jnp.zeros((64, NZ), F32)], 0), EY + 2, EY + 3)
    out_ref[pl.ds(BLK - 1, DEVS, stride=BLK), :] = jnp.zeros((DEVS, 128), F32)


def filter_kernel(
    dev_ref, rz_ref, rx_ref, ry_ref, in_ref, xh_ref, xl_ref, yh_ref, yl_ref, yth_ref, ytl_ref, eyh_ref, eyl_ref,
    ex2h_ref, ex2l_ref, exh_ref, exl_ref, out_ref,
    th_ref, tl_ref, eh_ref, el_ref, wh_ref, wl_ref, uh_ref, ul_ref, ry2_ref,
):
    rows = RY * BLK
    parts = ([], [])
    for j in range(RY // 2):
        load = [
            jnp.concatenate(
                [
                    in_ref[pl.ds((2 * j + i) * BLK + EY + col, RX, stride=rows), :]
                    for col in range(3)
                ],
                0,
            )
            for i in range(2)
        ]
        a, b = swap(load[0], load[1])
        parts[0].append(a)
        parts[1].append(b)
    edge = split(jnp.concatenate([jnp.concatenate(p, 1) for p in parts], 0))

    def edges(i, carry):
        at = pl.ds(pl.multiple_of(i * CHUNK, CHUNK), CHUNK)
        high, low = split(mm3((eyh_ref[at, :], eyl_ref[at, :]), edge, NT))
        eh_ref[at, :] = high
        el_ref[at, :] = low
        return carry

    lax.fori_loop(0, NY // CHUNK, edges, 0)

    for j in range(RX // 2):
        pair = split(
            jnp.concatenate(
                [in_ref[2 * j * rows : (2 * j + 1) * rows, :], in_ref[(2 * j + 1) * rows : (2 * j + 2) * rows, :]], 1
            )
        )

        def forward_y(i, carry):
            at = pl.ds(pl.multiple_of(i * CHUNK, CHUNK), CHUNK)
            turned = mm3((yh_ref[at, :], yl_ref[at, :]), pair)
            for z, part in enumerate(swap(turned[:, :128], turned[:, 128:])):
                high, low = split(part)
                th_ref[z, at, 128 * j : 128 * (j + 1)] = high
                tl_ref[z, at, 128 * j : 128 * (j + 1)] = low
            return carry

        lax.fori_loop(0, NY // CHUNK, forward_y, 0)

    ry2_ref[...] = jnp.transpose(jnp.broadcast_to(ry_ref[...], (128, NY)))
    dev = dev_ref[0]
    scale = 4.0 / (NX * NY * NZ)

    def middle(i, carry):
        at = pl.ds(pl.multiple_of(i * CHUNK, CHUNK), CHUNK)
        table = (xh_ref[...], xl_ref[...])
        back = []
        for z in range(2):
            coeffs = mm3((th_ref[z, at, :], tl_ref[z, at, :]), table) + mm3(
                (eh_ref[at, :], el_ref[at, :]), (ex2h_ref[z], ex2l_ref[z])
            )
            rate = 1.0 + rz_ref[dev + z * DEVS]
            weighted = []
            for k in range(NX // 128):
                lanes = slice(128 * k, 128 * (k + 1))
                denom = ry2_ref[at, :] + (rx_ref[:, lanes] + rate)
                weighted.append(coeffs[:, lanes] * (scale / (denom * denom)))
            weighted = split(jnp.concatenate(weighted, 1))
            wh_ref[z, at, :] = weighted[0]
            wl_ref[z, at, :] = weighted[1]
            back.append(mm3(weighted, table))
        for k in range(NX // 128):
            lanes = slice(128 * k, 128 * (k + 1))
            for n, part in enumerate(swap(back[0][:, lanes], back[1][:, lanes])):
                high, low = split(part)
                uh_ref[at, (2 * k + n) * 128 : (2 * k + n + 1) * 128] = high
                ul_ref[at, (2 * k + n) * 128 : (2 * k + n + 1) * 128] = low
        return carry

    lax.fori_loop(0, NY // CHUNK, middle, 0)

    for j in range(RX // 2):
        lanes = slice(256 * j, 256 * (j + 1))
        field = (uh_ref[:, lanes], ul_ref[:, lanes])

        def backward_y(i, carry):
            at = pl.ds(pl.multiple_of(i * 160, 160), 160)
            turned = mm3((yth_ref[at, :], ytl_ref[at, :]), field)
            for n in range(2):
                out_ref[pl.ds(pl.multiple_of((2 * j + n) * rows + i * 160, 160), 160), :] = turned[
                    :, 128 * n : 128 * (n + 1)
                ]
            return carry

        lax.fori_loop(0, rows // 160, backward_y, 0)

    edge_x = (exh_ref[...], exl_ref[...])
    tall = split(
        jnp.concatenate([mm3(edge_x, (wh_ref[z], wl_ref[z]), NT) for z in range(2)], 0)
    )
    for j in range(RY // 2):
        lanes = slice(128 * j, 128 * (j + 1))
        wide = mm3(tall, (eyh_ref[:, lanes], eyl_ref[:, lanes]))
        for n, part in enumerate(swap(wide[:24], wide[24:])):
            for col in range(3):
                out_ref[pl.ds((2 * j + n) * BLK + EY + col, RX, stride=rows), :] = part[
                    8 * col : 8 * col + 8
                ]


def sample_kernel(
    grid_ref, counts_ref, val_ref, noise_ref, frac_ref, xy_ref, z_ref, in_ref, tzh_ref, tzl_ref, out_ref,
    taps_ref, pad_ref, boxh_ref, boxl_ref,
):
    tiles = val_ref.shape[0]
    fill_taps(frac_ref, taps_ref)
    table = (tzh_ref[...], tzl_ref[...])

    def get(first, second):
        a = in_ref[pl.ds(first, DEVS, stride=BLK), :]
        b = in_ref[pl.ds(second, DEVS, stride=BLK), :]
        turned = jnp.concatenate(swap(a, b), 0)
        return mm3(split(jnp.transpose(turned)), table)

    for pair in range(SY // 2):
        y = 2 * pair
        rows = get(y, y + 1)
        pad_ref[y, 1:65, :] = rows[:64]
        pad_ref[y + 1, 1:65, :] = rows[64:]
    for first, at in ((EY, (0, 1)), (EY + 2, (2,))):
        rows = get(first, first + 1)
        for n, col in enumerate(at):
            pad_ref[:, HALO[col][0], :] = rows[64 * n : 64 * n + SY]
    pad_ref[:, 67:72, :] = jnp.zeros((SY, 5, NZ), F32)
    for gx in range(BX // TILE):
        for y in range(SY):
            high, low = split(pad_ref[y, TILE * gx : TILE * gx + 16, :])
            boxh_ref[gx, y] = high
            boxl_ref[gx, y] = low

    slots = lax.broadcasted_iota(jnp.int32, (1, PTS), 1)

    def step(t, carry):
        taps, cell_x, cell_y, cell_z = tile_rows(t, taps_ref, xy_ref, z_ref)
        wide_x = window(cell_x, taps[0:4], 16)
        wide_y = window(cell_y, taps[4:8], 16)
        col = split(column(cell_z, taps[8:12]))
        g = grid_ref[t]
        gx = g // GROW
        gy = g - gx * GROW
        place = pl.ds(gy * TILE, BOX)
        high = boxh_ref[gx, place].reshape(BOX * 16, NZ)
        low = boxl_ref[gx, place].reshape(BOX * 16, NZ)
        along = mm(high, jnp.concatenate(col, 1))
        along = along[:, :PTS] + along[:, PTS:] + mm(low, col[0])
        total = wide_y[0:1] * along[0:16]
        for q in range(1, BOX):
            total = total + wide_y[q : q + 1] * along[16 * q : 16 * q + 16]
        sampled = jnp.sum(total * wide_x, axis=0, keepdims=True)
        row = pl.ds(t, 1)
        out_ref[row, :] = jnp.where(
            slots < counts_ref[t], noise_ref[row, :] * val_ref[row, :] + sampled, 0.0
        )
        return carry

    lax.fori_loop(0, tiles, step, 0)


def body(values, noise, fractions, cell_xy, cell_z, tile_grid, counts, rate_x, rate_y, rate_z):
    tiles = values.shape[0]
    tab = {name: (jnp.asarray(pair[0]), jnp.asarray(pair[1])) for name, pair in tables().items()}
    vmem = pl.BlockSpec(memory_space=pltpu.VMEM)
    smem = pl.BlockSpec(memory_space=pltpu.SMEM)
    limit = pltpu.CompilerParams(vmem_limit_bytes=56 << 20)
    exchange = jax.ShapeDtypeStruct((DEVS * BLK, 128), F32)

    sent = pl.pallas_call(
        spread_kernel,
        out_shape=exchange,
        in_specs=[smem] * 2 + [vmem] * 6,
        out_specs=vmem,
        scratch_shapes=[pltpu.VMEM((12, tiles, PTS), F32), pltpu.VMEM((SY, SX, NZ), F32)],
        compiler_params=limit,
    )(tile_grid, counts, values, fractions, cell_xy, cell_z, *tab["z"])

    def regroup(array):
        array = array.reshape(DEVS, BLK, 128)
        array = lax.all_to_all(array, ("gx", "gy"), split_axis=0, concat_axis=0, tiled=True)
        return array.reshape(DEVS * BLK, 128)

    planes = regroup(sent)
    dev = (lax.axis_index("gx") * RY + lax.axis_index("gy")).astype(jnp.int32).reshape(1)
    filtered = pl.pallas_call(
        filter_kernel,
        out_shape=exchange,
        in_specs=[smem] * 2 + [vmem] * 15,
        out_specs=vmem,
        scratch_shapes=[
            pltpu.VMEM((2, NY, NX), BF),
            pltpu.VMEM((2, NY, NX), BF),
            pltpu.VMEM((NY, 48), BF),
            pltpu.VMEM((NY, 48), BF),
            pltpu.VMEM((2, NY, NX), BF),
            pltpu.VMEM((2, NY, NX), BF),
            pltpu.VMEM((NY, 2 * NX), BF),
            pltpu.VMEM((NY, 2 * NX), BF),
            pltpu.VMEM((NY, 128), F32),
        ],
        compiler_params=limit,
    )(
        dev, rate_z, rate_x.reshape(1, NX), rate_y.reshape(1, NY), planes,
        *tab["x"], *tab["y"], *tab["yt"], *tab["ey"], *tab["ex2"], *tab["ex"],
    )
    smooth = regroup(filtered)

    return pl.pallas_call(
        sample_kernel,
        out_shape=jax.ShapeDtypeStruct((tiles, PTS), F32),
        in_specs=[smem] * 2 + [vmem] * 8,
        out_specs=vmem,
        scratch_shapes=[
            pltpu.VMEM((12, tiles, PTS), F32),
            pltpu.VMEM((SY, SX, NZ), F32),
            pltpu.VMEM((BX // TILE, SY, 16, NZ), BF),
            pltpu.VMEM((BX // TILE, SY, 16, NZ), BF),
        ],
        compiler_params=limit,
    )(tile_grid, counts, values, noise, fractions, cell_xy, cell_z, smooth, *tab["z"])


def solution(mesh):
    points = P(("gx", "gy"), None)
    triple = P(None, ("gx", "gy"), None)
    flat = P(("gx", "gy"))
    in_specs = (points, points, triple, triple, points, flat, flat, P(), P(), P())
    return jax.shard_map(body, mesh=mesh, in_specs=in_specs, out_specs=points, check_vma=False)
```

time: 649 us -> 261 us (0.40); the launches traced: 640 us -> 261 us
  matrix products: 366 us -> 0 us
  Pallas kernels: 0 us -> 172 us
  local copies, waits for them, and re-layouts: 78.6 us -> 1.51 us
  blocking collectives: 93.1 us -> 40.8 us
  other arithmetic: 37.3 us -> 0 us
  starting transfers between devices: 23.2 us -> 11.5 us
    dot_general x22 -> x0, matrix products: 366 us -> none  [the longest x4 130 us: sample_step(): jnp.einsum('bpq,bqz->bpz', plane_weight, local_boxes, precision=PRECISE)]
    pallas_call x0 -> x3, Pallas kernels: none -> 172 us  [the longest x1 75.7 us: body(): pl.pallas_call(spread_kernel, out_shape=exchange, in_specs=[smem] * 2 + [...]
    all_to_all x3 -> x1, blocking collectives: 93.1 us -> 40.8 us  [regroup(): lax.all_to_all(array, ('gx', 'gy'), split_axis=0, concat_axis=0, tiled=True)]
    all_to_all x7 -> x0, local copies, waits for them, and re-layouts: 17.8 us -> none  [the longest x2 10.7 us: body(): lax.all_to_all(slabs, 'gy', split_axis=2, concat_axis=1, tiled=True)]
    ppermute x8 -> x0, starting transfers between devices: 16.4 us -> none  [the longest x4 9.16 us: extended(): lax.ppermute(lax.slice_in_dim(block, 0, width, axis=dim), axis, backward)]
    unnamed x23 -> x2, local copies, waits for them, and re-layouts: 17.5 us -> 1.51 us
    reshape x4 -> x0, local copies, waits for them, and re-layouts: 15.9 us -> none  [the longest x1 6.47 us: body(): accum.reshape(rows_x, rows_y, box_side, box_side, depth)]
    ppermute x8 -> x0, waiting for transfers between devices: 14.8 us -> none  [the longest x4 9.75 us: extended(): lax.ppermute(lax.slice_in_dim(block, block.shape[dim] - width, None, axis...]
  transfers between devices with their start and end apart: 9 -> 1, of which waited for: 7 -> 1; matrix products, arithmetic and copies ran while one was open for 0% -> 0% of each run, Pallas kernels for 0% -> 0%
where the time goes in v1:
time: 261 us
  Pallas kernels  172 us (66%)
  blocking collectives  40.8 us (16%)
  waiting for transfers between devices  35.1 us (13%)
  starting transfers between devices  11.5 us (4%)
    pallas_call x1, Pallas kernels, body(): pl.pallas_call(spread_kernel, out_shape=exchange, in_specs=[smem] * 2 + [...  75.7 us
    pallas_call x1, Pallas kernels, body(): pl.pallas_call(sample_kernel, out_shape=jax.ShapeDtypeStruct((tiles, PTS)...  70 us
    all_to_all x1, blocking collectives, regroup(): lax.all_to_all(array, ('gx', 'gy'), split_axis=0, concat_axis=0, tiled=True)  40.8 us
    all_to_all x1, waiting for transfers between devices, regroup(): lax.all_to_all(array, ('gx', 'gy'), split_axis=0, concat_axis=0, tiled=True)  35.1 us
    pallas_call x1, Pallas kernels, body(): pl.pallas_call(filter_kernel, out_shape=exchange, in_specs=[smem] * 2 + [...  26.3 us
    all_to_all x1, starting transfers between devices, regroup(): lax.all_to_all(array, ('gx', 'gy'), split_axis=0, concat_axis=0, tiled=True)  11.5 us
  transfers between devices with their start and end apart: 1, of which 1 were waited for; matrix products, arithmetic and copies ran while one was open for 0% of the time, Pallas kernels for 0%

profile of v1, /device:TPU:1, one launch (start us, length us, event | category | flops | bytes accessed | tf_op | source)
XLA Modules:
  0.0 261.1 jit_solution(18032294563450070901)
XLA Ops:
  0.0 75.7 %shard_map.226 = f32[5120,128]{1,0:T(8,128)} custom-call(s32[256]{0:T(256)} %grid_ref.3, s32[256]{0:T(256)} %counts_ref.3, f32[256,128]{1,0:T(8,128)} %val_ref.3, f32[3,256,128]{2,1,0:T(8,128)} %frac_ref.3, s32[2,256,128]{2,1,0:T(8,128)} %xy_ref.3, s32[256,128]{1,0:T(8,128)} %z_ref.3, bf16[256,256]{1,0:T(8,128)(2,1)} %constant.39.clone.tzh_ref, ...), custom_call_target="tpu_custom_call" | custom-call | tf_op jit(solution)/shard_map/pallas_call | solution.py:370
  75.7 11.5 %all-to-all-start = ((f32[128,40,128]{2,1,0:T(8,128)}), f32[128,40,128]{2,1,0:T(8,128)S(1)}, u32[]{:S(2)}, u32[]{:S(2)}) async-start(f32[128,40,128]{2,1,0:T(8,128)} %bitcast.7), calls=%async_computation | async-start | bytes 5242880 | tf_op jit(solution)/shard_map/all_to_all | solution.py:381
  87.2 35.1 %all-to-all-done = f32[128,40,128]{2,1,0:T(8,128)S(1)} async-done(((f32[128,40,128]{2,1,0:T(8,128)}), f32[128,40,128]{2,1,0:T(8,128)S(1)}, u32[]{:S(2)}, u32[]{:S(2)}) %all-to-all-start) | async-done | bytes 2621472 | tf_op jit(solution)/shard_map/all_to_all | solution.py:381
  122.3 0.0 copy-start
  122.3 1.5 copy-done
  123.9 26.3 %shard_map.227 = f32[5120,128]{1,0:T(8,128)} custom-call(s32[1]{0:T(128)} %bitcast.dev_ref, f32[256]{0:T(256)} %rz_ref.1, f32[1,512]{1,0:T(1,128)} %bitcast.11, f32[1,512]{1,0:T(1,128)} %bitcast.12, f32[5120,128]{1,0:T(8,128)} %bitcast.9, bf16[512,512]{1,0:T(8,128)(2,1)} %constant.41.clone.xh_ref, bf16[512,512]{1,0:T(8,128)(2,1)} %constant.42.clone.xl_ref, ...), custom_call_target="tpu_custom_call" | custom-call | tf_op jit(solution)/shard_map/pallas_call | solution.py:386
  150.2 40.8 %all_to_all.10 = f32[128,40,128]{2,1,0:T(8,128)} all-to-all(f32[128,40,128]{2,1,0:T(8,128)} %bitcast.10), channel_id=1, replica_groups=mesh['gx'=8,'gy'=16] {'gx','gy'}, dimensions={0} | all-to-all | bytes 5242880 | tf_op jit(solution)/shard_map/all_to_all | solution.py:381
  191.0 70.0 %shard_map.228 = f32[256,128]{1,0:T(8,128)} custom-call(s32[256]{0:T(256)} %grid_ref.3, s32[256]{0:T(256)} %counts_ref.3, f32[256,128]{1,0:T(8,128)} %val_ref.3, f32[256,128]{1,0:T(8,128)} %noise_ref.1, f32[3,256,128]{2,1,0:T(8,128)} %frac_ref.3, s32[2,256,128]{2,1,0:T(8,128)} %xy_ref.3, s32[256,128]{1,0:T(8,128)} %z_ref.3, f32[5120,128]{1,0:T(8,128)} %bitcast.8, ...), custom_call_target="tpu_custom_call" | custom-call | tf_op jit(solution)/shard_map/pallas_call | solution.py:409
Async XLA Ops:
  75.7 46.6 %all-to-all-start = ((f32[128,40,128]{2,1,0:T(8,128)}), f32[128,40,128]{2,1,0:T(8,128)S(1)}, u32[]{:S(2)}, u32[]{:S(2)}) async-start(f32[128,40,128]{2,1,0:T(8,128)} %bitcast.7), calls=%async_computation | async-start | bytes 5242880 | tf_op jit(solution)/shard_map/all_to_all | solution.py:381
  122.3 1.5 copy-start

commit v2 on v1

--- a/solution.py
+++ b/solution.py
@@ -21,7 +21,7 @@
 BOX = 11
 BLK = 40
 HALO = ((0, -1), (65, 64), (66, 65))
-CHUNK = 128
+CHUNK = 256
 
 BF = jnp.bfloat16
 F32 = jnp.float32
@@ -107,17 +107,24 @@
     )
 
 
-def fill_taps(frac_ref, taps_ref):
+def fill_taps(frac_ref, z_ref, taps_ref, cells_ref):
     tiles = frac_ref.shape[1]
 
     def step(i, carry):
         rows = pl.ds(pl.multiple_of(i * 8, 8), 8)
-        for axis in range(3):
+        for axis in range(2):
             for offset, tap in enumerate(cubic_taps(frac_ref[axis, rows, :])):
                 taps_ref[axis * 4 + offset, rows, :] = tap
+        for offset, tap in enumerate(cubic_taps(frac_ref[2, rows, :])):
+            high, low = split(tap)
+            cell = (z_ref[rows, :] + (offset - 1)) & (NZ - 1)
+            taps_ref[8 + offset, rows, :] = cell.astype(F32)
+            taps_ref[12 + offset, rows, :] = high.astype(F32)
+            taps_ref[16 + offset, rows, :] = low.astype(F32)
         return carry
 
     lax.fori_loop(0, tiles // 8, step, 0)
+    cells_ref[...] = lax.broadcasted_iota(jnp.int32, (NZ, PTS), 0).astype(F32).astype(BF)
 
 
 def window(start, taps, length):
@@ -128,37 +135,37 @@
     return weights
 
 
-def column(start, taps):
-    delta = (lax.broadcasted_iota(jnp.int32, (NZ, PTS), 0) - (start - 1)) & (NZ - 1)
-    weights = jnp.where(delta == 0, taps[0], 0.0)
-    for offset in range(1, 4):
-        weights = jnp.where(delta == offset, taps[offset], weights)
-    return weights
-
-
-def tile_rows(t, taps_ref, xy_ref, z_ref):
-    row = pl.ds(t, 1)
-    taps = [taps_ref[k, row, :] for k in range(12)]
-    return taps, xy_ref[0, row, :], xy_ref[1, row, :], z_ref[row, :]
+def column(row, taps_ref, cells_ref):
+    cells = cells_ref[...]
+    high = low = jnp.zeros((NZ, PTS), BF)
+    for k in range(4):
+        hit = cells == taps_ref[8 + k, row, :].astype(BF)
+        high = jnp.where(hit, taps_ref[12 + k, row, :].astype(BF), high)
+        low = jnp.where(hit, taps_ref[16 + k, row, :].astype(BF), low)
+    return high, low
 
 
 def spread_kernel(
-    grid_ref, counts_ref, val_ref, frac_ref, xy_ref, z_ref, tzh_ref, tzl_ref, out_ref, taps_ref, pad_ref
+    grid_ref, counts_ref, val_ref, frac_ref, xy_ref, z_ref, tzh_ref, tzl_ref, out_ref,
+    taps_ref, cells_ref, pad_ref,
 ):
     tiles = val_ref.shape[0]
-    fill_taps(frac_ref, taps_ref)
+    fill_taps(frac_ref, z_ref, taps_ref, cells_ref)
     pad_ref[...] = jnp.zeros_like(pad_ref)
     slots = lax.broadcasted_iota(jnp.int32, (1, PTS), 1)
 
     def step(t, carry):
-        taps, cell_x, cell_y, cell_z = tile_rows(t, taps_ref, xy_ref, z_ref)
-        source = jnp.where(slots < counts_ref[t], val_ref[pl.ds(t, 1), :], 0.0)
-        wide_x = window(cell_x, taps[0:4], 16)
-        wide_y = window(cell_y, [tap * source for tap in taps[4:8]], 16)
+        row = pl.ds(t, 1)
+        taps = [taps_ref[k, row, :] for k in range(8)]
+        source = jnp.where(slots < counts_ref[t], val_ref[row, :], 0.0)
+        wide_x = window(xy_ref[0, row, :], taps[0:4], 16)
+        wide_y = window(xy_ref[1, row, :], [tap * source for tap in taps[4:8]], 16)
         plane = jnp.concatenate([wide_y[q : q + 1] * wide_x for q in range(BOX)], 0)
-        plane = split(plane)
-        col = split(column(cell_z, taps[8:12]))
-        box = mm3(plane, col, NT)
+        high, low = split(plane)
+        col = column(row, taps_ref, cells_ref)
+        box = mm(
+            jnp.concatenate([high, low, high], 1), jnp.concatenate([col[0], col[0], col[1]], 1), NT
+        )
         g = grid_ref[t]
         gx = g // GROW
         gy = g - gx * GROW
@@ -167,7 +174,7 @@
             pad_ref[gy * TILE + q, place, :] += box[q * 16 : q * 16 + 16]
         return carry
 
-    lax.fori_loop(0, tiles, step, 0)
+    lax.fori_loop(0, tiles, step, 0, unroll=16)
 
     table = (tzh_ref[...], tzl_ref[...])
 
@@ -220,7 +227,7 @@
         el_ref[at, :] = low
         return carry
 
-    lax.fori_loop(0, NY // CHUNK, edges, 0)
+    lax.fori_loop(0, NY // CHUNK, edges, 0, unroll=True)
 
     for j in range(RX // 2):
         pair = split(
@@ -238,7 +245,7 @@
                 tl_ref[z, at, 128 * j : 128 * (j + 1)] = low
             return carry
 
-        lax.fori_loop(0, NY // CHUNK, forward_y, 0)
+        lax.fori_loop(0, NY // CHUNK, forward_y, 0, unroll=True)
 
     ry2_ref[...] = jnp.transpose(jnp.broadcast_to(ry_ref[...], (128, NY)))
     dev = dev_ref[0]
@@ -270,7 +277,7 @@
                 ul_ref[at, (2 * k + n) * 128 : (2 * k + n + 1) * 128] = low
         return carry
 
-    lax.fori_loop(0, NY // CHUNK, middle, 0)
+    lax.fori_loop(0, NY // CHUNK, middle, 0, unroll=True)
 
     for j in range(RX // 2):
         lanes = slice(256 * j, 256 * (j + 1))
@@ -285,7 +292,7 @@
                 ]
             return carry
 
-        lax.fori_loop(0, rows // 160, backward_y, 0)
+        lax.fori_loop(0, rows // 160, backward_y, 0, unroll=True)
 
     edge_x = (exh_ref[...], exl_ref[...])
     tall = split(
@@ -303,10 +310,10 @@
 
 def sample_kernel(
     grid_ref, counts_ref, val_ref, noise_ref, frac_ref, xy_ref, z_ref, in_ref, tzh_ref, tzl_ref, out_ref,
-    taps_ref, pad_ref, boxh_ref, boxl_ref,
+    taps_ref, cells_ref, pad_ref, boxh_ref, boxl_ref,
 ):
     tiles = val_ref.shape[0]
-    fill_taps(frac_ref, taps_ref)
+    fill_taps(frac_ref, z_ref, taps_ref, cells_ref)
     table = (tzh_ref[...], tzl_ref[...])
 
     def get(first, second):
@@ -334,29 +341,29 @@
     slots = lax.broadcasted_iota(jnp.int32, (1, PTS), 1)
 
     def step(t, carry):
-        taps, cell_x, cell_y, cell_z = tile_rows(t, taps_ref, xy_ref, z_ref)
-        wide_x = window(cell_x, taps[0:4], 16)
-        wide_y = window(cell_y, taps[4:8], 16)
-        col = split(column(cell_z, taps[8:12]))
+        row = pl.ds(t, 1)
+        taps = [taps_ref[k, row, :] for k in range(8)]
+        wide_x = window(xy_ref[0, row, :], taps[0:4], 16)
+        wide_y = window(xy_ref[1, row, :], taps[4:8], 16)
+        col = column(row, taps_ref, cells_ref)
         g = grid_ref[t]
         gx = g // GROW
         gy = g - gx * GROW
         place = pl.ds(gy * TILE, BOX)
         high = boxh_ref[gx, place].reshape(BOX * 16, NZ)
         low = boxl_ref[gx, place].reshape(BOX * 16, NZ)
-        along = mm(high, jnp.concatenate(col, 1))
-        along = along[:, :PTS] + along[:, PTS:] + mm(low, col[0])
+        along = mm(jnp.concatenate([high, low], 0), jnp.concatenate(col, 1))
+        along = along[: BOX * 16, :PTS] + along[: BOX * 16, PTS:] + along[BOX * 16 :, :PTS]
         total = wide_y[0:1] * along[0:16]
         for q in range(1, BOX):
             total = total + wide_y[q : q + 1] * along[16 * q : 16 * q + 16]
         sampled = jnp.sum(total * wide_x, axis=0, keepdims=True)
-        row = pl.ds(t, 1)
         out_ref[row, :] = jnp.where(
             slots < counts_ref[t], noise_ref[row, :] * val_ref[row, :] + sampled, 0.0
         )
         return carry
 
-    lax.fori_loop(0, tiles, step, 0)
+    lax.fori_loop(0, tiles, step, 0, unroll=16)
 
 
 def body(values, noise, fractions, cell_xy, cell_z, tile_grid, counts, rate_x, rate_y, rate_z):
@@ -372,7 +379,7 @@
         out_shape=exchange,
         in_specs=[smem] * 2 + [vmem] * 6,
         out_specs=vmem,
-        scratch_shapes=[pltpu.VMEM((12, tiles, PTS), F32), pltpu.VMEM((SY, SX, NZ), F32)],
+        scratch_shapes=[pltpu.VMEM((20, tiles, PTS), F32), pltpu.VMEM((NZ, PTS), BF), pltpu.VMEM((SY, SX, NZ), F32)],
         compiler_params=limit,
     )(tile_grid, counts, values, fractions, cell_xy, cell_z, *tab["z"])
 
@@ -412,7 +419,8 @@
         in_specs=[smem] * 2 + [vmem] * 8,
         out_specs=vmem,
         scratch_shapes=[
-            pltpu.VMEM((12, tiles, PTS), F32),
+            pltpu.VMEM((20, tiles, PTS), F32),
+            pltpu.VMEM((NZ, PTS), BF),
             pltpu.VMEM((SY, SX, NZ), F32),
             pltpu.VMEM((BX // TILE, SY, 16, NZ), BF),
             pltpu.VMEM((BX // TILE, SY, 16, NZ), BF),

time: 261 us -> 187 us (0.72)
  Pallas kernels: 172 us -> 97.3 us
    pallas_call x1, Pallas kernels: 70 us -> 32.3 us  [body(): pl.pallas_call(sample_kernel, out_shape=jax.ShapeDtypeStruct((tiles, PTS)...]
    pallas_call x1, Pallas kernels: 75.7 us -> 47.8 us  [body(): pl.pallas_call(spread_kernel, out_shape=exchange, in_specs=[smem] * 2 + [...]
    pallas_call x1, Pallas kernels: 26.3 us -> 17.1 us  [body(): pl.pallas_call(filter_kernel, out_shape=exchange, in_specs=[smem] * 2 + [...]
where the time goes in v2:
time: 187 us; the launch traced here: 186 us
  Pallas kernels  97.3 us (52%)
  blocking collectives  40.9 us (22%)
  waiting for transfers between devices  35.1 us (19%)
  starting transfers between devices  11.5 us (6%)
    pallas_call x1, Pallas kernels, body(): pl.pallas_call(spread_kernel, out_shape=exchange, in_specs=[smem] * 2 + [...  47.8 us
    all_to_all x1, blocking collectives, regroup(): lax.all_to_all(array, ('gx', 'gy'), split_axis=0, concat_axis=0, tiled=True)  40.9 us
    all_to_all x1, waiting for transfers between devices, regroup(): lax.all_to_all(array, ('gx', 'gy'), split_axis=0, concat_axis=0, tiled=True)  35.1 us
    pallas_call x1, Pallas kernels, body(): pl.pallas_call(sample_kernel, out_shape=jax.ShapeDtypeStruct((tiles, PTS)...  32.3 us
    pallas_call x1, Pallas kernels, body(): pl.pallas_call(filter_kernel, out_shape=exchange, in_specs=[smem] * 2 + [...  17.1 us
    all_to_all x1, starting transfers between devices, regroup(): lax.all_to_all(array, ('gx', 'gy'), split_axis=0, concat_axis=0, tiled=True)  11.5 us
  transfers between devices with their start and end apart: 1, of which 1 were waited for; matrix products, arithmetic and copies ran while one was open for 0% of the time, Pallas kernels for 0%

profile of v2, /device:TPU:1, one launch (start us, length us, event | category | flops | bytes accessed | tf_op | source)
XLA Modules:
  0.0 186.3 jit_solution(2125019779450818052)
XLA Ops:
  0.0 47.8 %shard_map.226 = f32[5120,128]{1,0:T(8,128)} custom-call(s32[256]{0:T(256)} %grid_ref.3, s32[256]{0:T(256)} %counts_ref.3, f32[256,128]{1,0:T(8,128)} %val_ref.3, f32[3,256,128]{2,1,0:T(8,128)} %frac_ref.3, s32[2,256,128]{2,1,0:T(8,128)} %xy_ref.3, s32[256,128]{1,0:T(8,128)} %z_ref.3, bf16[256,256]{1,0:T(8,128)(2,1)} %constant.39.clone.tzh_ref, ...), custom_call_target="tpu_custom_call" | custom-call | tf_op jit(solution)/shard_map/pallas_call | solution.py:377
  47.8 11.5 %all-to-all-start = ((f32[128,40,128]{2,1,0:T(8,128)}), f32[128,40,128]{2,1,0:T(8,128)S(1)}, u32[]{:S(2)}, u32[]{:S(2)}) async-start(f32[128,40,128]{2,1,0:T(8,128)} %bitcast.7), calls=%async_computation | async-start | bytes 5242880 | tf_op jit(solution)/shard_map/all_to_all | solution.py:388
  59.3 35.1 %all-to-all-done = f32[128,40,128]{2,1,0:T(8,128)S(1)} async-done(((f32[128,40,128]{2,1,0:T(8,128)}), f32[128,40,128]{2,1,0:T(8,128)S(1)}, u32[]{:S(2)}, u32[]{:S(2)}) %all-to-all-start) | async-done | bytes 2621472 | tf_op jit(solution)/shard_map/all_to_all | solution.py:388
  94.5 0.0 copy-start
  94.5 1.5 copy-done
  96.0 17.1 %shard_map.227 = f32[5120,128]{1,0:T(8,128)} custom-call(s32[1]{0:T(128)} %bitcast.dev_ref, f32[256]{0:T(256)} %rz_ref.1, f32[1,512]{1,0:T(1,128)} %bitcast.11, f32[1,512]{1,0:T(1,128)} %bitcast.12, f32[5120,128]{1,0:T(8,128)} %bitcast.9, bf16[512,512]{1,0:T(8,128)(2,1)} %constant.41.clone.xh_ref, bf16[512,512]{1,0:T(8,128)(2,1)} %constant.42.clone.xl_ref, ...), custom_call_target="tpu_custom_call" | custom-call | tf_op jit(solution)/shard_map/pallas_call | solution.py:393
  113.1 40.9 %all_to_all.10 = f32[128,40,128]{2,1,0:T(8,128)} all-to-all(f32[128,40,128]{2,1,0:T(8,128)} %bitcast.10), channel_id=1, replica_groups=mesh['gx'=8,'gy'=16] {'gx','gy'}, dimensions={0} | all-to-all | bytes 5242880 | tf_op jit(solution)/shard_map/all_to_all | solution.py:388
  153.9 32.3 %shard_map.228 = f32[256,128]{1,0:T(8,128)} custom-call(s32[256]{0:T(256)} %grid_ref.3, s32[256]{0:T(256)} %counts_ref.3, f32[256,128]{1,0:T(8,128)} %val_ref.3, f32[256,128]{1,0:T(8,128)} %noise_ref.1, f32[3,256,128]{2,1,0:T(8,128)} %frac_ref.3, s32[2,256,128]{2,1,0:T(8,128)} %xy_ref.3, s32[256,128]{1,0:T(8,128)} %z_ref.3, f32[5120,128]{1,0:T(8,128)} %bitcast.8, ...), custom_call_target="tpu_custom_call" | custom-call | tf_op jit(solution)/shard_map/pallas_call | solution.py:416
Async XLA Ops:
  47.8 46.6 %all-to-all-start = ((f32[128,40,128]{2,1,0:T(8,128)}), f32[128,40,128]{2,1,0:T(8,128)S(1)}, u32[]{:S(2)}, u32[]{:S(2)}) async-start(f32[128,40,128]{2,1,0:T(8,128)} %bitcast.7), calls=%async_computation | async-start | bytes 5242880 | tf_op jit(solution)/shard_map/all_to_all | solution.py:388
  94.5 1.5 copy-start

commit v3 on v2

v3 whole, which is shorter than its diff:
```python
import math

import jax
import jax.numpy as jnp
import ml_dtypes
import numpy as np
from jax import lax
from jax.experimental import pallas as pl
from jax.experimental.pallas import tpu as pltpu
from jax.sharding import PartitionSpec as P

NX, NY, NZ = 512, 512, 256
TILE = 8
PTS = 128
RX, RY = 8, 16
DEVS = RX * RY
BX, BY = NX // RX, NY // RY
GROW = BY // TILE
EY = BY + 3
SY, SX = 36, 72
BOX = 11
BLK = 40
HALO = ((0, -1), (65, 64), (66, 65))
CHUNK = 128

BF = jnp.bfloat16
F32 = jnp.float32
NN = (((1,), (0,)), ((), ()))
NT = (((1,), (1,)), ((), ()))


def halves(table):
    table = np.asarray(table, np.float32)
    high = table.astype(ml_dtypes.bfloat16)
    low = (table - high.astype(np.float32)).astype(ml_dtypes.bfloat16)
    return high, low


def cas(rows, columns, length):
    phase = np.outer(np.asarray(rows, np.int64), np.asarray(columns, np.int64)) % length
    angle = phase * (2.0 * math.pi / length)
    return np.cos(angle) + np.sin(angle)


def tables():
    half = np.arange(NX // 2)
    line = np.arange(EY) - 1
    full_y = cas(np.arange(NY), (np.arange(RY)[:, None] * BY + line[None, :]).reshape(-1) % NY, NY)
    full_y = full_y.reshape(NY, RY, EY)
    rows_y = np.zeros((NY // 2, RY, BLK))
    rows_y[:, :, :EY] = full_y[: NY // 2]
    rows_y = rows_y.reshape(NY // 2, RY * BLK // 2, 2)
    edge_y = np.zeros((NY, RY, 64))
    edge_y[:, :, :EY] = full_y
    edge_y = edge_y.reshape(NY, RY * 64)
    order = np.concatenate([2 * half, 2 * half + 1])
    edge_x = cas(np.concatenate([np.arange(RX) * BX + offset for _, offset in HALO]) % NX, order, NX)
    edge_two = np.zeros((2, 48, NX))
    edge_two[0, :24] = edge_x
    edge_two[1, 24:] = edge_x
    table_x = np.concatenate([cas(half, 2 * half, NX), cas(half, 2 * half + 1, NX)], 1)
    wide = np.concatenate([table_x, edge_two.reshape(96, NX), edge_x, np.zeros((8, NX))])
    return {
        "z": np.concatenate(halves(cas(np.arange(NZ), np.arange(NZ), NZ))),
        "x": np.stack(halves(wide)),
        "y": np.stack(halves(rows_y.transpose(2, 0, 1))),
        "yt": np.stack(halves(rows_y.transpose(2, 1, 0))),
        "ey": np.stack(halves(edge_y)),
    }


EX2 = NX // 2
EX = EX2 + 96


def split(value):
    high = value.astype(BF)
    return high, (value - high.astype(F32)).astype(BF)


def mm(a, b, dims=NN):
    return lax.dot_general(a, b, dims, preferred_element_type=F32)


def mm3(a, b, dims=NN):
    return mm(a[0], b[0], dims) + (mm(a[0], b[1], dims) + mm(a[1], b[0], dims))


def cubic_taps(fraction):
    square = fraction * fraction
    cubed = square * fraction
    return (
        -0.5 * cubed + square - 0.5 * fraction,
        1.5 * cubed - 2.5 * square + 1.0,
        -1.5 * cubed + 2.0 * square + 0.5 * fraction,
        0.5 * cubed - 0.5 * square,
    )


def low_lanes(shape):
    return lax.broadcasted_iota(jnp.int32, shape, 1) < 64


def swap(a, b):
    low = low_lanes(a.shape)
    return (
        jnp.where(low, a, pltpu.roll(b, 64, 1)),
        jnp.where(low, pltpu.roll(a, 64, 1), b),
    )


def fill_taps(frac_ref, z_ref, taps_ref):
    tiles = frac_ref.shape[1]

    def step(i, carry):
        rows = pl.ds(pl.multiple_of(i * 8, 8), 8)
        for axis in range(2):
            for offset, tap in enumerate(cubic_taps(frac_ref[axis, rows, :])):
                taps_ref[axis * 4 + offset, rows, :] = tap
        for offset, tap in enumerate(cubic_taps(frac_ref[2, rows, :])):
            high, low = split(tap)
            taps_ref[8 + offset, rows, :] = high.astype(F32)
            taps_ref[12 + offset, rows, :] = low.astype(F32)
        first = (z_ref[rows, :] + (NZ - 1)) & (NZ - 1)
        taps_ref[16, rows, :] = (first & 15).astype(F32)
        taps_ref[17, rows, :] = (first >> 4).astype(F32)
        return carry

    lax.fori_loop(0, tiles // 8, step, 0)


def window(start, taps, length):
    delta = lax.broadcasted_iota(jnp.int32, (length, PTS), 0) - start
    weights = jnp.where(delta == 0, taps[0], 0.0)
    for offset in range(1, 4):
        weights = jnp.where(delta == offset, taps[offset], weights)
    return weights


def column(row, taps_ref):
    low_place = taps_ref[16, row, :].astype(BF)
    run = taps_ref[17, row, :].astype(BF)
    taps = [taps_ref[8 + k, row, :].astype(BF) for k in range(8)]
    pair = []
    for part in range(2):
        delta = (lax.broadcasted_iota(jnp.int32, (16, PTS), 0) + 16 * part).astype(F32).astype(BF) - low_place
        high = low = jnp.zeros((16, PTS), BF)
        for k in range(4):
            hit = delta == k
            high = jnp.where(hit, taps[k], high)
            low = jnp.where(hit, taps[4 + k], low)
        pair.append((high, low))
    wide_run = jnp.broadcast_to(run, (16, PTS))
    zero = jnp.zeros((16, PTS), BF)
    highs, lows = [], []
    before = wide_run == NZ // 16 - 1
    for i in range(NZ // 16):
        here = wide_run == i
        highs.append(jnp.where(here, pair[0][0], jnp.where(before, pair[1][0], zero)))
        lows.append(jnp.where(here, pair[0][1], jnp.where(before, pair[1][1], zero)))
        before = here
    return jnp.concatenate(highs, 0), jnp.concatenate(lows, 0)


def spread_kernel(
    grid_ref, counts_ref, val_ref, frac_ref, xy_ref, z_ref, tz_ref, out_ref,
    taps_ref, pad_ref,
):
    tiles = val_ref.shape[0]
    fill_taps(frac_ref, z_ref, taps_ref)
    pad_ref[...] = jnp.zeros_like(pad_ref)
    slots = lax.broadcasted_iota(jnp.int32, (1, PTS), 1)

    def step(t, carry):
        row = pl.ds(t, 1)
        taps = [taps_ref[k, row, :] for k in range(8)]
        source = jnp.where(slots < counts_ref[t], val_ref[row, :], 0.0)
        wide_x = window(xy_ref[0, row, :], taps[0:4], 16)
        wide_y = window(xy_ref[1, row, :], [tap * source for tap in taps[4:8]], 16)
        plane = jnp.concatenate([wide_y[q : q + 1] * wide_x for q in range(BOX)], 0)
        high, low = split(plane)
        col = column(row, taps_ref)
        box = mm(
            jnp.concatenate([high, low, high], 1), jnp.concatenate([col[0], col[0], col[1]], 1), NT
        )
        g = grid_ref[t]
        gx = g // GROW
        gy = g - gx * GROW
        place = pl.ds(pl.multiple_of(gx * TILE, TILE), 16)
        for q in range(BOX):
            pad_ref[gy * TILE + q, place, :] += box[q * 16 : q * 16 + 16]
        return carry

    lax.fori_loop(0, tiles, step, 0, unroll=64)

    table = (tz_ref[:NZ], tz_ref[NZ:])

    def put(rows, first, second):
        turned = mm3(table, split(rows), NT)
        a, b = swap(turned[:DEVS], turned[DEVS:])
        out_ref[pl.ds(first, DEVS, stride=BLK), :] = a
        if second is not None:
            out_ref[pl.ds(second, DEVS, stride=BLK), :] = b

    for pair in range(SY // 2):
        y = 2 * pair
        rows = jnp.concatenate([pad_ref[y, 1:65, :], pad_ref[y + 1, 1:65, :]], 0)
        put(rows, y, y + 1 if y + 1 < EY else None)
    edges = [
        jnp.concatenate([pad_ref[:, at, :], jnp.zeros((64 - SY, NZ), F32)], 0) for at, _ in HALO
    ]
    put(jnp.concatenate([edges[0], edges[1]], 0), EY, EY + 1)
    put(jnp.concatenate([edges[2], jnp.zeros((64, NZ), F32)], 0), EY + 2, EY + 3)
    out_ref[pl.ds(BLK - 1, DEVS, stride=BLK), :] = jnp.zeros((DEVS, 128), F32)


def filter_kernel(
    dev_ref, rz_ref, rx_ref, ry_ref, in_ref, x_hbm, y_hbm, yt_hbm, ey_hbm, out_ref,
    x_ref, y_ref, yt_ref, ey_ref, th_ref, tl_ref, eh_ref, el_ref, wh_ref, wl_ref, uh_ref, ul_ref, ry2_ref, sems,
):
    copies = [
        pltpu.make_async_copy(source, target, sems.at[n])
        for n, (source, target) in enumerate(
            ((y_hbm, y_ref), (ey_hbm, ey_ref), (x_hbm, x_ref), (yt_hbm, yt_ref))
        )
    ]
    for copy in copies:
        copy.start()
    rows = RY * BLK
    half = NX // 2
    ry2_ref[...] = jnp.transpose(jnp.broadcast_to(ry_ref[...], (128, NY)))

    copies[0].wait()
    for j in range(RX // 4):
        sides = []
        for pair in (j, j + RX // 4):
            odd = []
            for parity in range(2):
                part = split(
                    jnp.concatenate(
                        [in_ref[pl.ds((2 * pair + n) * rows + parity, rows // 2, stride=2), :] for n in range(2)], 1
                    )
                )
                odd.append(mm3((y_ref[0, parity], y_ref[1, parity]), part))
            turned = (odd[1] + odd[0], odd[1] - odd[0])
            sides.append([swap(t[:, :128], t[:, 128:]) for t in turned])
        for k in range(2):
            at = slice(half * k, half * (k + 1))
            for z in range(2):
                first, second = sides[0][k][z], sides[1][k][z]
                for n, part in enumerate((first + second, first - second)):
                    lanes = slice(half * n + 128 * j, half * n + 128 * (j + 1))
                    high, low = split(part)
                    th_ref[z, at, lanes] = high
                    tl_ref[z, at, lanes] = low

    parts = ([], [])
    for j in range(RY // 2):
        load = [
            jnp.concatenate(
                [
                    in_ref[pl.ds((2 * j + i) * BLK + EY + col, RX, stride=rows), :]
                    for col in range(3)
                ],
                0,
            )
            for i in range(2)
        ]
        a, b = swap(load[0], load[1])
        parts[0].append(a)
        parts[1].append(b)
    edge = split(jnp.concatenate([jnp.concatenate(p, 1) for p in parts], 0))
    copies[1].wait()
    for i in range(2):
        at = slice(half * i, half * (i + 1))
        high, low = split(mm3((ey_ref[0, at, :], ey_ref[1, at, :]), edge, NT))
        eh_ref[at, :] = high
        el_ref[at, :] = low

    copies[2].wait()
    dev = dev_ref[0]
    scale = 4.0 / (NX * NY * NZ)
    table = [
        tuple(x_ref[part, :half, half * n : half * (n + 1)] for part in range(2)) for n in range(2)
    ]
    for i in range(half // CHUNK):
        fields = []
        for k in range(2):
            at = slice(half * k + CHUNK * i, half * k + CHUNK * (i + 1))
            back = []
            for z in range(2):
                rate = 1.0 + rz_ref[dev + z * DEVS]
                sums = []
                for n in range(2):
                    lanes = slice(half * n, half * (n + 1))
                    ends = slice(EX2 + 48 * z, EX2 + 48 * z + 48)
                    coeffs = mm3((th_ref[z, at, lanes], tl_ref[z, at, lanes]), table[n]) + mm3(
                        (eh_ref[at, :], el_ref[at, :]), (x_ref[0, ends, lanes], x_ref[1, ends, lanes])
                    )
                    weighted = []
                    for q in range(2):
                        cut = slice(half * n + 128 * q, half * n + 128 * (q + 1))
                        denom = ry2_ref[at, :] + (rx_ref[:, cut] + rate)
                        weighted.append(coeffs[:, 128 * q : 128 * (q + 1)] * (scale / (denom * denom)))
                    weighted = split(jnp.concatenate(weighted, 1))
                    wh_ref[z, at, lanes] = weighted[0]
                    wl_ref[z, at, lanes] = weighted[1]
                    sums.append(mm3(weighted, table[n], NT))
                back.append((sums[0] + sums[1], sums[0] - sums[1]))
            fields.append(back)
        for side in range(2):
            for q in range(2):
                lanes = slice(128 * q, 128 * (q + 1))
                low_k = swap(fields[0][0][side][:, lanes], fields[0][1][side][:, lanes])
                high_k = swap(fields[1][0][side][:, lanes], fields[1][1][side][:, lanes])
                for n in range(2):
                    block = 4 * side + 2 * q + n
                    for parity, value in enumerate((low_k[n] + high_k[n], low_k[n] - high_k[n])):
                        high, low = split(value)
                        uh_ref[parity, CHUNK * i : CHUNK * (i + 1), 128 * block : 128 * (block + 1)] = high
                        ul_ref[parity, CHUNK * i : CHUNK * (i + 1), 128 * block : 128 * (block + 1)] = low

    copies[3].wait()
    for j in range(RX // 2):
        lanes = slice(256 * j, 256 * (j + 1))
        for parity in range(2):
            field = (uh_ref[1 - parity, :, lanes], ul_ref[1 - parity, :, lanes])
            turned = mm3((yt_ref[0, parity], yt_ref[1, parity]), field)
            for n in range(2):
                out_ref[pl.ds((2 * j + n) * rows + parity, rows // 2, stride=2), :] = turned[
                    :, 128 * n : 128 * (n + 1)
                ]

    ends = slice(EX, EX + 24)
    tall = split(
        jnp.concatenate(
            [
                mm3((x_ref[0, ends, :], x_ref[1, ends, :]), (wh_ref[z], wl_ref[z]), NT)
                for z in range(2)
            ],
            0,
        )
    )
    for j in range(RY // 2):
        lanes = slice(128 * j, 128 * (j + 1))
        wide = mm3(tall, (ey_ref[0, :, lanes], ey_ref[1, :, lanes]))
        for n, part in enumerate(swap(wide[:24], wide[24:])):
            for col in range(3):
                out_ref[pl.ds((2 * j + n) * BLK + EY + col, RX, stride=rows), :] = part[
                    8 * col : 8 * col + 8
                ]


def sample_kernel(
    grid_ref, counts_ref, val_ref, noise_ref, frac_ref, xy_ref, z_ref, in_ref, tz_ref, out_ref,
    taps_ref, pad_ref, boxh_ref, boxl_ref,
):
    tiles = val_ref.shape[0]
    fill_taps(frac_ref, z_ref, taps_ref)
    table = (tz_ref[:NZ], tz_ref[NZ:])

    def get(first, second):
        a = in_ref[pl.ds(first, DEVS, stride=BLK), :]
        b = in_ref[pl.ds(second, DEVS, stride=BLK), :]
        turned = jnp.concatenate(swap(a, b), 0)
        return mm3(split(jnp.transpose(turned)), table)

    for pair in range(SY // 2):
        y = 2 * pair
        rows = get(y, y + 1)
        pad_ref[y, 1:65, :] = rows[:64]
        pad_ref[y + 1, 1:65, :] = rows[64:]
    for first, at in ((EY, (0, 1)), (EY + 2, (2,))):
        rows = get(first, first + 1)
        for n, col in enumerate(at):
            pad_ref[:, HALO[col][0], :] = rows[64 * n : 64 * n + SY]
    pad_ref[:, 67:72, :] = jnp.zeros((SY, 5, NZ), F32)
    for gx in range(BX // TILE):
        for y in range(SY):
            high, low = split(pad_ref[y, TILE * gx : TILE * gx + 16, :])
            boxh_ref[gx, y] = high
            boxl_ref[gx, y] = low

    slots = lax.broadcasted_iota(jnp.int32, (1, PTS), 1)

    def step(t, carry):
        row = pl.ds(t, 1)
        taps = [taps_ref[k, row, :] for k in range(8)]
        wide_x = window(xy_ref[0, row, :], taps[0:4], 16)
        wide_y = window(xy_ref[1, row, :], taps[4:8], 16)
        col = column(row, taps_ref)
        g = grid_ref[t]
        gx = g // GROW
        gy = g - gx * GROW
        place = pl.ds(gy * TILE, BOX)
        high = boxh_ref[gx, place].reshape(BOX * 16, NZ)
        low = boxl_ref[gx, place].reshape(BOX * 16, NZ)
        along = mm(jnp.concatenate([high, low], 0), jnp.concatenate(col, 1))
        along = along[: BOX * 16, :PTS] + along[: BOX * 16, PTS:] + along[BOX * 16 :, :PTS]
        total = wide_y[0:1] * along[0:16]
        for q in range(1, BOX):
            total = total + wide_y[q : q + 1] * along[16 * q : 16 * q + 16]
        sampled = jnp.sum(total * wide_x, axis=0, keepdims=True)
        out_ref[row, :] = jnp.where(
            slots < counts_ref[t], noise_ref[row, :] * val_ref[row, :] + sampled, 0.0
        )
        return carry

    lax.fori_loop(0, tiles, step, 0, unroll=64)


def body(values, noise, fractions, cell_xy, cell_z, tile_grid, counts, rate_x, rate_y, rate_z):
    tiles = values.shape[0]
    tab = {name: jnp.asarray(table) for name, table in tables().items()}
    vmem = pl.BlockSpec(memory_space=pltpu.VMEM)
    smem = pl.BlockSpec(memory_space=pltpu.SMEM)
    large = pltpu.CompilerParams(vmem_limit_bytes=56 << 20)
    limit = pltpu.CompilerParams(vmem_limit_bytes=32 << 20)
    exchange = jax.ShapeDtypeStruct((DEVS * BLK, 128), F32)

    sent = pl.pallas_call(
        spread_kernel,
        out_shape=exchange,
        in_specs=[smem] * 2 + [vmem] * 5,
        out_specs=vmem,
        scratch_shapes=[pltpu.VMEM((18, tiles, PTS), F32), pltpu.VMEM((SY, SX, NZ), F32)],
        compiler_params=large,
    )(tile_grid, counts, values, fractions, cell_xy, cell_z, tab["z"])

    def regroup(array):
        array = array.reshape(DEVS, BLK, 128)
        array = lax.all_to_all(array, ("gx", "gy"), split_axis=0, concat_axis=0, tiled=True)
        return array.reshape(DEVS * BLK, 128)

    planes = regroup(sent)
    dev = (lax.axis_index("gx") * RY + lax.axis_index("gy")).astype(jnp.int32).reshape(1)
    by_parity = rate_x.reshape(NX // 2, 2).T.reshape(1, NX)
    hbm = pl.BlockSpec(memory_space=pltpu.HBM)
    names = ("x", "y", "yt", "ey")
    filtered = pl.pallas_call(
        filter_kernel,
        out_shape=exchange,
        in_specs=[smem] * 2 + [vmem] * 3 + [hbm] * 4,
        out_specs=vmem,
        scratch_shapes=[pltpu.VMEM(tab[name].shape, BF) for name in names]
        + [
            pltpu.VMEM((2, NY, NX), BF),
            pltpu.VMEM((2, NY, NX), BF),
            pltpu.VMEM((NY, 48), BF),
            pltpu.VMEM((NY, 48), BF),
            pltpu.VMEM((2, NY, NX), BF),
            pltpu.VMEM((2, NY, NX), BF),
            pltpu.VMEM((2, NY // 2, 2 * NX), BF),
            pltpu.VMEM((2, NY // 2, 2 * NX), BF),
            pltpu.VMEM((NY, 128), F32),
            pltpu.SemaphoreType.DMA((4,)),
        ],
        compiler_params=limit,
    )(dev, rate_z, by_parity, rate_y.reshape(1, NY), planes, *[tab[name] for name in names])
    smooth = regroup(filtered)

    return pl.pallas_call(
        sample_kernel,
        out_shape=jax.ShapeDtypeStruct((tiles, PTS), F32),
        in_specs=[smem] * 2 + [vmem] * 7,
        out_specs=vmem,
        scratch_shapes=[
            pltpu.VMEM((18, tiles, PTS), F32),
            pltpu.VMEM((SY, SX, NZ), F32),
            pltpu.VMEM((BX // TILE, SY, 16, NZ), BF),
            pltpu.VMEM((BX // TILE, SY, 16, NZ), BF),
        ],
        compiler_params=limit,
    )(tile_grid, counts, values, noise, fractions, cell_xy, cell_z, smooth, tab["z"])


def solution(mesh):
    points = P(("gx", "gy"), None)
    triple = P(None, ("gx", "gy"), None)
    flat = P(("gx", "gy"))
    in_specs = (points, points, triple, triple, points, flat, flat, P(), P(), P())
    return jax.shard_map(body, mesh=mesh, in_specs=in_specs, out_specs=points, check_vma=False)
```

time: 187 us -> 145 us (0.78)
  Pallas kernels: 97.3 us -> 54.2 us
  local copies, waits for them, and re-layouts: 1.51 us -> 4.09 us
    pallas_call x1, Pallas kernels: 47.8 us -> 25.9 us  [body(): pl.pallas_call(spread_kernel, out_shape=exchange, in_specs=[smem] * 2 + [...]
    pallas_call x1, Pallas kernels: 32.3 us -> 16.8 us  [body(): pl.pallas_call(sample_kernel, out_shape=jax.ShapeDtypeStruct((tiles, PTS)...]
    pallas_call x1, Pallas kernels: 17.1 us -> 11.5 us  [body(): pl.pallas_call(filter_kernel, out_shape=exchange, in_specs=[smem] * 2 + [...]
    unnamed x2 -> x31, local copies, waits for them, and re-layouts: 1.51 us -> 3.88 us
where the time goes in v3:
time: 145 us
  Pallas kernels  54.2 us (37%)
  blocking collectives  39.8 us (27%)
  waiting for transfers between devices  34.9 us (24%)
  starting transfers between devices  11.6 us (8%)
  local copies, waits for them, and re-layouts  4.09 us (3%)
    all_to_all x1, blocking collectives, regroup(): lax.all_to_all(array, ('gx', 'gy'), split_axis=0, concat_axis=0, tiled=True)  39.8 us
    all_to_all x1, waiting for transfers between devices, regroup(): lax.all_to_all(array, ('gx', 'gy'), split_axis=0, concat_axis=0, tiled=True)  34.9 us
    pallas_call x1, Pallas kernels, body(): pl.pallas_call(spread_kernel, out_shape=exchange, in_specs=[smem] * 2 + [...  25.9 us
    pallas_call x1, Pallas kernels, body(): pl.pallas_call(sample_kernel, out_shape=jax.ShapeDtypeStruct((tiles, PTS)...  16.8 us
    all_to_all x1, starting transfers between devices, regroup(): lax.all_to_all(array, ('gx', 'gy'), split_axis=0, concat_axis=0, tiled=True)  11.6 us
    pallas_call x1, Pallas kernels, body(): pl.pallas_call(filter_kernel, out_shape=exchange, in_specs=[smem] * 2 + [...  11.5 us
    unnamed x31, local copies, waits for them, and re-layouts  3.88 us
  transfers between devices with their start and end apart: 1, of which 1 were waited for; matrix products, arithmetic and copies ran while one was open for 0% of the time, Pallas kernels for 0%

profile of v3, /device:TPU:1, one launch (start us, length us, event | category | flops | bytes accessed | tf_op | source)
XLA Modules:
  0.0 144.7 jit_solution(7390169218261174816)
XLA Ops:
  0.0 25.9 %shard_map.145 = f32[5120,128]{1,0:T(8,128)} custom-call(s32[256]{0:T(256)} %grid_ref.3, s32[256]{0:T(256)} %counts_ref.3, f32[256,128]{1,0:T(8,128)} %val_ref.3, f32[3,256,128]{2,1,0:T(8,128)} %frac_ref.3, s32[2,256,128]{2,1,0:T(8,128)} %xy_ref.3, s32[256,128]{1,0:T(8,128)} %z_ref.3, bf16[512,256]{1,0:T(8,128)(2,1)} %constant.21.clone.tz_ref), custom_call_target="tpu_custom_call" | custom-call | tf_op jit(solution)/shard_map/pallas_call | solution.py:421
  25.9 0.0 copy-start.14
  25.9 0.0 copy-start.4
  25.9 0.0 copy-start.12
  25.9 0.0 copy-start.13
  26.0 11.6 %all-to-all-start = ((f32[128,40,128]{2,1,0:T(8,128)}), f32[128,40,128]{2,1,0:T(8,128)S(1)}, u32[]{:S(2)}, u32[]{:S(2)}) async-start(f32[128,40,128]{2,1,0:T(8,128)} %bitcast.15), calls=%async_computation | async-start | bytes 5242880 | tf_op jit(solution)/shard_map/all_to_all | solution.py:432
  37.5 0.0 copy-done.14
  37.5 0.1 reshape.25
  37.7 0.1 copy.16
  37.8 34.9 %all-to-all-done = f32[128,40,128]{2,1,0:T(8,128)S(1)} async-done(((f32[128,40,128]{2,1,0:T(8,128)}), f32[128,40,128]{2,1,0:T(8,128)S(1)}, u32[]{:S(2)}, u32[]{:S(2)}) %all-to-all-start) | async-done | bytes 2621472 | tf_op jit(solution)/shard_map/all_to_all | solution.py:432
  72.6 0.0 copy-done.4
  72.6 0.0 copy-done.12
  72.6 0.0 copy-done.13
  72.7 0.0 copy-start
  72.7 1.6 %copy-done = bf16[2,512,1024]{2,1,0:T(8,128)(2,1)S(1)} copy-done((bf16[2,512,1024]{2,1,0:T(8,128)(2,1)S(1)}, bf16[2,512,1024]{2,1,0:T(8,128)(2,1)}, u32[]{:S(2)}) %copy-start) | copy-done | bytes 2097176
  74.2 0.0 copy-start.5
  74.3 1.1 copy-done.5
  75.4 0.0 copy-start.6
  75.4 1.1 copy-done.6
  76.5 11.5 %shard_map.146 = f32[5120,128]{1,0:T(8,128)S(1)} custom-call(s32[1]{0:T(128)} %bitcast.dev_ref, f32[256]{0:T(256)S(1)} %copy-done.13, f32[1,512]{1,0:T(1,128)S(1)} %bitcast.13, f32[1,512]{1,0:T(1,128)S(1)} %bitcast.14, f32[5120,128]{1,0:T(8,128)S(1)} %bitcast.10, bf16[2,384,512]{2,1,0:T(8,128)(2,1)S(1)} %copy-done.4, bf16[2,2,256,320]{3,2,1,0:T(8,128)(2,1)S(1)} %copy-done.5, ...), custom_call_target="tpu_custom_call" | custom-call | tf_op jit(solution)/shard_map/pallas_call | solution.py:440
  88.0 0.0 copy-start.1
  88.0 0.0 copy-start.2
  88.0 0.0 copy-start.3
  88.0 0.0 copy-start.7
  88.0 0.0 copy-start.8
  88.1 0.0 copy-start.9
  88.1 0.0 copy-start.10
  88.1 0.0 copy-start.11
  88.1 39.8 %all_to_all.10 = f32[128,40,128]{2,1,0:T(8,128)S(1)} all-to-all(f32[128,40,128]{2,1,0:T(8,128)S(1)} %bitcast.11), channel_id=1, replica_groups=mesh['gx'=8,'gy'=16] {'gx','gy'}, dimensions={0} | all-to-all | bytes 5242880 | tf_op jit(solution)/shard_map/all_to_all | solution.py:432
  127.9 0.0 copy-done.1
  127.9 0.0 copy-done.2
  127.9 0.0 copy-done.3
  127.9 0.0 copy-done.7
  127.9 0.0 copy-done.8
  127.9 0.0 copy-done.9
  127.9 0.0 copy-done.10
  127.9 0.0 copy-done.11
  127.9 16.8 %shard_map.147 = f32[256,128]{1,0:T(8,128)} custom-call(s32[256]{0:T(256)S(1)} %copy-done.10, s32[256]{0:T(256)S(1)} %copy-done.11, f32[256,128]{1,0:T(8,128)S(1)} %copy-done.7, f32[256,128]{1,0:T(8,128)S(1)} %copy-done.9, f32[3,256,128]{2,1,0:T(8,128)S(1)} %copy-done.1, s32[2,256,128]{2,1,0:T(8,128)S(1)} %copy-done.2, s32[256,128]{1,0:T(8,128)S(1)} %copy-done.8, ...), custom_call_target="tpu_custom_call" | custom-call | tf_op jit(solution)/shard_map/pallas_call | solution.py:462
  (1 shorter events, 0.0 us)
Async XLA Ops:
  25.9 11.6 %copy-start.14 = (f32[512]{0:T(512)S(1)}, f32[512]{0:T(512)}, u32[]{:S(2)}) copy-start(f32[512]{0:T(512)} %param.22) | copy-start | bytes 6148
  25.9 46.7 %copy-start.4 = (bf16[2,384,512]{2,1,0:T(8,128)(2,1)S(1)}, bf16[2,384,512]{2,1,0:T(8,128)(2,1)}, u32[]{:S(2)}) copy-start(bf16[2,384,512]{2,1,0:T(8,128)(2,1)} %constant.22.clone.x_hbm) | copy-start | bytes 2359300
  25.9 46.7 %copy-start.12 = (f32[512]{0:T(512)S(1)}, f32[512]{0:T(512)}, u32[]{:S(2)}) copy-start(f32[512]{0:T(512)} %param.23) | copy-start | bytes 6148
  25.9 46.7 %copy-start.13 = (f32[256]{0:T(256)S(1)}, f32[256]{0:T(256)}, u32[]{:S(2)}) copy-start(f32[256]{0:T(256)} %rz_ref.1) | copy-start | bytes 3076
  26.0 46.7 %all-to-all-start = ((f32[128,40,128]{2,1,0:T(8,128)}), f32[128,40,128]{2,1,0:T(8,128)S(1)}, u32[]{:S(2)}, u32[]{:S(2)}) async-start(f32[128,40,128]{2,1,0:T(8,128)} %bitcast.15), calls=%async_computation | async-start | bytes 5242880 | tf_op jit(solution)/shard_map/all_to_all | solution.py:432
  72.7 1.6 %copy-start = (bf16[2,512,1024]{2,1,0:T(8,128)(2,1)S(1)}, bf16[2,512,1024]{2,1,0:T(8,128)(2,1)}, u32[]{:S(2)}) copy-start(bf16[2,512,1024]{2,1,0:T(8,128)(2,1)} %constant.25.clone.ey_hbm) | copy-start | bytes 6291460
  74.2 1.1 copy-start.5
  75.4 1.1 copy-start.6
  88.0 39.9 %copy-start.1 = (f32[3,256,128]{2,1,0:T(8,128)S(1)}, f32[3,256,128]{2,1,0:T(8,128)}, u32[]{:S(2)}) copy-start(f32[3,256,128]{2,1,0:T(8,128)} %frac_ref.3) | copy-start | bytes 1179652
  88.0 39.9 %copy-start.2 = (s32[2,256,128]{2,1,0:T(8,128)S(1)}, s32[2,256,128]{2,1,0:T(8,128)}, u32[]{:S(2)}) copy-start(s32[2,256,128]{2,1,0:T(8,128)} %xy_ref.3) | copy-start | bytes 786436
  88.0 39.9 %copy-start.3 = (bf16[512,256]{1,0:T(8,128)(2,1)S(1)}, bf16[512,256]{1,0:T(8,128)(2,1)}, u32[]{:S(2)}) copy-start(bf16[512,256]{1,0:T(8,128)(2,1)} %constant.21.clone.tz_ref) | copy-start | bytes 786436
  88.0 39.9 %copy-start.7 = (f32[256,128]{1,0:T(8,128)S(1)}, f32[256,128]{1,0:T(8,128)}, u32[]{:S(2)}) copy-start(f32[256,128]{1,0:T(8,128)} %val_ref.3) | copy-start | bytes 393220
  88.0 39.9 %copy-start.8 = (s32[256,128]{1,0:T(8,128)S(1)}, s32[256,128]{1,0:T(8,128)}, u32[]{:S(2)}) copy-start(s32[256,128]{1,0:T(8,128)} %z_ref.3) | copy-start | bytes 393220
  88.1 39.9 %copy-start.9 = (f32[256,128]{1,0:T(8,128)S(1)}, f32[256,128]{1,0:T(8,128)}, u32[]{:S(2)}) copy-start(f32[256,128]{1,0:T(8,128)} %noise_ref.1) | copy-start | bytes 393220
  88.1 39.9 %copy-start.10 = (s32[256]{0:T(256)S(1)}, s32[256]{0:T(256)}, u32[]{:S(2)}) copy-start(s32[256]{0:T(256)} %grid_ref.3) | copy-start | bytes 3076
  88.1 39.9 %copy-start.11 = (s32[256]{0:T(256)S(1)}, s32[256]{0:T(256)}, u32[]{:S(2)}) copy-start(s32[256]{0:T(256)} %counts_ref.3) | copy-start | bytes 3076

commit v4 on v3

--- a/solution.py
+++ b/solution.py
@@ -27,6 +27,7 @@
 F32 = jnp.float32
 NN = (((1,), (0,)), ((), ()))
 NT = (((1,), (1,)), ((), ()))
+TN = (((0,), (0,)), ((), ()))
 
 
 def halves(table):
@@ -63,14 +64,13 @@
     return {
         "z": np.concatenate(halves(cas(np.arange(NZ), np.arange(NZ), NZ))),
         "x": np.stack(halves(wide)),
-        "y": np.stack(halves(rows_y.transpose(2, 0, 1))),
-        "yt": np.stack(halves(rows_y.transpose(2, 1, 0))),
-        "ey": np.stack(halves(edge_y)),
+        "ey": np.stack(halves(np.concatenate([edge_y, rows_y.transpose(2, 0, 1).reshape(NY, -1)], 1))),
     }
 
 
 EX2 = NX // 2
 EX = EX2 + 96
+EDGE = RY * 64
 
 
 def split(value):
@@ -195,42 +195,34 @@
 
     table = (tz_ref[:NZ], tz_ref[NZ:])
 
-    def put(rows, first, second):
-        turned = mm3(table, split(rows), NT)
-        a, b = swap(turned[:DEVS], turned[DEVS:])
-        out_ref[pl.ds(first, DEVS, stride=BLK), :] = a
-        if second is not None:
-            out_ref[pl.ds(second, DEVS, stride=BLK), :] = b
-
-    for pair in range(SY // 2):
-        y = 2 * pair
-        rows = jnp.concatenate([pad_ref[y, 1:65, :], pad_ref[y + 1, 1:65, :]], 0)
-        put(rows, y, y + 1 if y + 1 < EY else None)
+    def put(blocks, first, last):
+        turned = mm3(table, split(jnp.concatenate(blocks, 0)), NT)
+        for pair in range(2):
+            lanes = slice(128 * pair, 128 * (pair + 1))
+            for n, part in enumerate(swap(turned[:DEVS, lanes], turned[DEVS:, lanes])):
+                if first + 2 * pair + n < last:
+                    out_ref[pl.ds(first + 2 * pair + n, DEVS, stride=BLK), :] = part
+
+    for first in range(0, SY, 4):
+        put([pad_ref[first + n, 1:65, :] for n in range(4)], first, EY)
     edges = [
         jnp.concatenate([pad_ref[:, at, :], jnp.zeros((64 - SY, NZ), F32)], 0) for at, _ in HALO
     ]
-    put(jnp.concatenate([edges[0], edges[1]], 0), EY, EY + 1)
-    put(jnp.concatenate([edges[2], jnp.zeros((64, NZ), F32)], 0), EY + 2, EY + 3)
+    put(edges + [jnp.zeros((64, NZ), F32)], EY, EY + 4)
     out_ref[pl.ds(BLK - 1, DEVS, stride=BLK), :] = jnp.zeros((DEVS, 128), F32)
 
 
 def filter_kernel(
-    dev_ref, rz_ref, rx_ref, ry_ref, in_ref, x_hbm, y_hbm, yt_hbm, ey_hbm, out_ref,
-    x_ref, y_ref, yt_ref, ey_ref, th_ref, tl_ref, eh_ref, el_ref, wh_ref, wl_ref, uh_ref, ul_ref, ry2_ref, sems,
+    dev_ref, rz_ref, rx_ref, ry_ref, in_ref, x_ref, ey_ref, out_ref,
+    th_ref, tl_ref, eh_ref, el_ref, wh_ref, wl_ref, uh_ref, ul_ref, ry2_ref,
 ):
-    copies = [
-        pltpu.make_async_copy(source, target, sems.at[n])
-        for n, (source, target) in enumerate(
-            ((y_hbm, y_ref), (ey_hbm, ey_ref), (x_hbm, x_ref), (yt_hbm, yt_ref))
-        )
-    ]
-    for copy in copies:
-        copy.start()
     rows = RY * BLK
     half = NX // 2
+    table_y = [
+        tuple(ey_ref[part, half * p : half * (p + 1), EDGE:] for part in range(2)) for p in range(2)
+    ]
     ry2_ref[...] = jnp.transpose(jnp.broadcast_to(ry_ref[...], (128, NY)))
 
-    copies[0].wait()
     for j in range(RX // 4):
         sides = []
         for pair in (j, j + RX // 4):
@@ -241,7 +233,7 @@
                         [in_ref[pl.ds((2 * pair + n) * rows + parity, rows // 2, stride=2), :] for n in range(2)], 1
                     )
                 )
-                odd.append(mm3((y_ref[0, parity], y_ref[1, parity]), part))
+                odd.append(mm3(table_y[parity], part))
             turned = (odd[1] + odd[0], odd[1] - odd[0])
             sides.append([swap(t[:, :128], t[:, 128:]) for t in turned])
         for k in range(2):
@@ -270,14 +262,12 @@
         parts[0].append(a)
         parts[1].append(b)
     edge = split(jnp.concatenate([jnp.concatenate(p, 1) for p in parts], 0))
-    copies[1].wait()
     for i in range(2):
         at = slice(half * i, half * (i + 1))
-        high, low = split(mm3((ey_ref[0, at, :], ey_ref[1, at, :]), edge, NT))
+        high, low = split(mm3((ey_ref[0, at, :EDGE], ey_ref[1, at, :EDGE]), edge, NT))
         eh_ref[at, :] = high
         el_ref[at, :] = low
 
-    copies[2].wait()
     dev = dev_ref[0]
     scale = 4.0 / (NX * NY * NZ)
     table = [
@@ -320,12 +310,11 @@
                         uh_ref[parity, CHUNK * i : CHUNK * (i + 1), 128 * block : 128 * (block + 1)] = high
                         ul_ref[parity, CHUNK * i : CHUNK * (i + 1), 128 * block : 128 * (block + 1)] = low
 
-    copies[3].wait()
     for j in range(RX // 2):
         lanes = slice(256 * j, 256 * (j + 1))
         for parity in range(2):
             field = (uh_ref[1 - parity, :, lanes], ul_ref[1 - parity, :, lanes])
-            turned = mm3((yt_ref[0, parity], yt_ref[1, parity]), field)
+            turned = mm3(table_y[parity], field, TN)
             for n in range(2):
                 out_ref[pl.ds((2 * j + n) * rows + parity, rows // 2, stride=2), :] = turned[
                     :, 128 * n : 128 * (n + 1)
@@ -435,15 +424,13 @@
     planes = regroup(sent)
     dev = (lax.axis_index("gx") * RY + lax.axis_index("gy")).astype(jnp.int32).reshape(1)
     by_parity = rate_x.reshape(NX // 2, 2).T.reshape(1, NX)
-    hbm = pl.BlockSpec(memory_space=pltpu.HBM)
-    names = ("x", "y", "yt", "ey")
+    names = ("x", "ey")
     filtered = pl.pallas_call(
         filter_kernel,
         out_shape=exchange,
-        in_specs=[smem] * 2 + [vmem] * 3 + [hbm] * 4,
+        in_specs=[smem] * 2 + [vmem] * 5,
         out_specs=vmem,
-        scratch_shapes=[pltpu.VMEM(tab[name].shape, BF) for name in names]
-        + [
+        scratch_shapes=[
             pltpu.VMEM((2, NY, NX), BF),
             pltpu.VMEM((2, NY, NX), BF),
             pltpu.VMEM((NY, 48), BF),
@@ -453,7 +440,6 @@
             pltpu.VMEM((2, NY // 2, 2 * NX), BF),
             pltpu.VMEM((2, NY // 2, 2 * NX), BF),
             pltpu.VMEM((NY, 128), F32),
-            pltpu.SemaphoreType.DMA((4,)),
         ],
         compiler_params=limit,
     )(dev, rate_z, by_parity, rate_y.reshape(1, NY), planes, *[tab[name] for name in names])

time: 145 us -> 142 us (0.979)
  local copies, waits for them, and re-layouts: 4.09 us -> 2.1 us
    unnamed x31 -> x27, local copies, waits for them, and re-layouts: 3.88 us -> 1.89 us
where the time goes in v4:
time: 142 us; the launch traced here: 141 us
  Pallas kernels  52.8 us (37%)
  blocking collectives  39.8 us (28%)
  waiting for transfers between devices  34.9 us (25%)
  starting transfers between devices  11.5 us (8%)
  local copies, waits for them, and re-layouts  2.1 us (1%)
    all_to_all x1, blocking collectives, regroup(): lax.all_to_all(array, ('gx', 'gy'), split_axis=0, concat_axis=0, tiled=True)  39.8 us
    all_to_all x1, waiting for transfers between devices, regroup(): lax.all_to_all(array, ('gx', 'gy'), split_axis=0, concat_axis=0, tiled=True)  34.9 us
    pallas_call x1, Pallas kernels, body(): pl.pallas_call(spread_kernel, out_shape=exchange, in_specs=[smem] * 2 + [...  25.2 us
    pallas_call x1, Pallas kernels, body(): pl.pallas_call(sample_kernel, out_shape=jax.ShapeDtypeStruct((tiles, PTS)...  17.3 us
    all_to_all x1, starting transfers between devices, regroup(): lax.all_to_all(array, ('gx', 'gy'), split_axis=0, concat_axis=0, tiled=True)  11.5 us
    pallas_call x1, Pallas kernels, body(): pl.pallas_call(filter_kernel, out_shape=exchange, in_specs=[smem] * 2 + [...  10.2 us
  transfers between devices with their start and end apart: 1, of which 1 were waited for; matrix products, arithmetic and copies ran while one was open for 0% of the time, Pallas kernels for 0%

profile of v4, /device:TPU:1, one launch (start us, length us, event | category | flops | bytes accessed | tf_op | source)
XLA Modules:
  0.0 141.2 jit_solution(9752676560263899601)
XLA Ops:
  0.0 25.2 %shard_map.127 = f32[5120,128]{1,0:T(8,128)} custom-call(s32[256]{0:T(256)} %grid_ref.3, s32[256]{0:T(256)} %counts_ref.3, f32[256,128]{1,0:T(8,128)} %val_ref.3, f32[3,256,128]{2,1,0:T(8,128)} %frac_ref.3, s32[2,256,128]{2,1,0:T(8,128)} %xy_ref.3, s32[256,128]{1,0:T(8,128)} %z_ref.3, bf16[512,256]{1,0:T(8,128)(2,1)} %constant.17.clone.tz_ref), custom_call_target="tpu_custom_call" | custom-call | tf_op jit(solution)/shard_map/pallas_call | solution.py:410
  25.2 0.0 copy-start.12
  25.2 0.0 copy-start.4
  25.2 0.0 copy-start.10
  25.2 0.0 copy-start.11
  25.2 11.5 %all-to-all-start = ((f32[128,40,128]{2,1,0:T(8,128)}), f32[128,40,128]{2,1,0:T(8,128)S(1)}, u32[]{:S(2)}, u32[]{:S(2)}) async-start(f32[128,40,128]{2,1,0:T(8,128)} %bitcast.15), calls=%async_computation | async-start | bytes 5242880 | tf_op jit(solution)/shard_map/all_to_all | solution.py:421
  36.7 0.0 copy-done.12
  36.7 0.1 reshape.25
  36.9 0.1 copy.14
  36.9 34.9 %all-to-all-done = f32[128,40,128]{2,1,0:T(8,128)S(1)} async-done(((f32[128,40,128]{2,1,0:T(8,128)}), f32[128,40,128]{2,1,0:T(8,128)S(1)}, u32[]{:S(2)}, u32[]{:S(2)}) %all-to-all-start) | async-done | bytes 2621472 | tf_op jit(solution)/shard_map/all_to_all | solution.py:421
  71.8 0.0 copy-done.4
  71.8 0.0 copy-done.10
  71.8 0.0 copy-done.11
  71.8 0.0 copy-start
  71.9 1.8 %copy-done = bf16[2,512,1344]{2,1,0:T(8,128)(2,1)S(1)} copy-done((bf16[2,512,1344]{2,1,0:T(8,128)(2,1)S(1)}, bf16[2,512,1344]{2,1,0:T(8,128)(2,1)}, u32[]{:S(2)}) %copy-start) | copy-done | bytes 2752536
  73.7 10.2 %shard_map.128 = f32[5120,128]{1,0:T(8,128)S(1)} custom-call(s32[1]{0:T(128)} %bitcast.dev_ref, f32[256]{0:T(256)S(1)} %copy-done.11, f32[1,512]{1,0:T(1,128)S(1)} %bitcast.13, f32[1,512]{1,0:T(1,128)S(1)} %bitcast.14, f32[5120,128]{1,0:T(8,128)S(1)} %bitcast.11, bf16[2,384,512]{2,1,0:T(8,128)(2,1)S(1)} %copy-done.4, bf16[2,512,1344]{2,1,0:T(8,128)(2,1)S(1)} %copy-done), custom_call_target="tpu_custom_call" | custom-call | tf_op jit(solution)/shard_map/pallas_call | solution.py:428
  83.9 0.0 copy-start.1
  83.9 0.0 copy-start.2
  83.9 0.0 copy-start.3
  84.0 0.0 copy-start.5
  84.0 0.0 copy-start.6
  84.0 0.0 copy-start.7
  84.0 0.0 copy-start.8
  84.0 0.0 copy-start.9
  84.0 39.8 %all_to_all.10 = f32[128,40,128]{2,1,0:T(8,128)S(1)} all-to-all(f32[128,40,128]{2,1,0:T(8,128)S(1)} %bitcast.12), channel_id=1, replica_groups=mesh['gx'=8,'gy'=16] {'gx','gy'}, dimensions={0} | all-to-all | bytes 5242880 | tf_op jit(solution)/shard_map/all_to_all | solution.py:421
  123.8 0.0 copy-done.1
  123.8 0.0 copy-done.2
  123.8 0.0 copy-done.3
  123.8 0.0 copy-done.5
  123.8 0.0 copy-done.6
  123.8 0.0 copy-done.7
  123.8 0.0 copy-done.8
  123.9 0.0 copy-done.9
  123.9 17.3 %shard_map.129 = f32[256,128]{1,0:T(8,128)} custom-call(s32[256]{0:T(256)S(1)} %copy-done.8, s32[256]{0:T(256)S(1)} %copy-done.9, f32[256,128]{1,0:T(8,128)S(1)} %copy-done.5, f32[256,128]{1,0:T(8,128)S(1)} %copy-done.7, f32[3,256,128]{2,1,0:T(8,128)S(1)} %copy-done.1, s32[2,256,128]{2,1,0:T(8,128)S(1)} %copy-done.2, s32[256,128]{1,0:T(8,128)S(1)} %copy-done.6, ...), custom_call_target="tpu_custom_call" | custom-call | tf_op jit(solution)/shard_map/pallas_call | solution.py:448
  (1 shorter events, 0.0 us)
Async XLA Ops:
  25.2 11.5 %copy-start.12 = (f32[512]{0:T(512)S(1)}, f32[512]{0:T(512)}, u32[]{:S(2)}) copy-start(f32[512]{0:T(512)} %param.20) | copy-start | bytes 6148
  25.2 46.6 %copy-start.4 = (bf16[2,384,512]{2,1,0:T(8,128)(2,1)S(1)}, bf16[2,384,512]{2,1,0:T(8,128)(2,1)}, u32[]{:S(2)}) copy-start(bf16[2,384,512]{2,1,0:T(8,128)(2,1)} %constant.18.clone.x_ref) | copy-start | bytes 2359300
  25.2 46.6 %copy-start.10 = (f32[512]{0:T(512)S(1)}, f32[512]{0:T(512)}, u32[]{:S(2)}) copy-start(f32[512]{0:T(512)} %param.21) | copy-start | bytes 6148
  25.2 46.6 %copy-start.11 = (f32[256]{0:T(256)S(1)}, f32[256]{0:T(256)}, u32[]{:S(2)}) copy-start(f32[256]{0:T(256)} %rz_ref.1) | copy-start | bytes 3076
  25.2 46.6 %all-to-all-start = ((f32[128,40,128]{2,1,0:T(8,128)}), f32[128,40,128]{2,1,0:T(8,128)S(1)}, u32[]{:S(2)}, u32[]{:S(2)}) async-start(f32[128,40,128]{2,1,0:T(8,128)} %bitcast.15), calls=%async_computation | async-start | bytes 5242880 | tf_op jit(solution)/shard_map/all_to_all | solution.py:421
  71.8 1.8 %copy-start = (bf16[2,512,1344]{2,1,0:T(8,128)(2,1)S(1)}, bf16[2,512,1344]{2,1,0:T(8,128)(2,1)}, u32[]{:S(2)}) copy-start(bf16[2,512,1344]{2,1,0:T(8,128)(2,1)} %constant.19.clone.ey_ref) | copy-start | bytes 8257540
  83.9 39.9 %copy-start.1 = (f32[3,256,128]{2,1,0:T(8,128)S(1)}, f32[3,256,128]{2,1,0:T(8,128)}, u32[]{:S(2)}) copy-start(f32[3,256,128]{2,1,0:T(8,128)} %frac_ref.3) | copy-start | bytes 1179652
  83.9 39.9 %copy-start.2 = (s32[2,256,128]{2,1,0:T(8,128)S(1)}, s32[2,256,128]{2,1,0:T(8,128)}, u32[]{:S(2)}) copy-start(s32[2,256,128]{2,1,0:T(8,128)} %xy_ref.3) | copy-start | bytes 786436
  83.9 39.9 %copy-start.3 = (bf16[512,256]{1,0:T(8,128)(2,1)S(1)}, bf16[512,256]{1,0:T(8,128)(2,1)}, u32[]{:S(2)}) copy-start(bf16[512,256]{1,0:T(8,128)(2,1)} %constant.17.clone.tz_ref) | copy-start | bytes 786436
  84.0 39.9 %copy-start.5 = (f32[256,128]{1,0:T(8,128)S(1)}, f32[256,128]{1,0:T(8,128)}, u32[]{:S(2)}) copy-start(f32[256,128]{1,0:T(8,128)} %val_ref.3) | copy-start | bytes 393220
  84.0 39.9 %copy-start.6 = (s32[256,128]{1,0:T(8,128)S(1)}, s32[256,128]{1,0:T(8,128)}, u32[]{:S(2)}) copy-start(s32[256,128]{1,0:T(8,128)} %z_ref.3) | copy-start | bytes 393220
  84.0 39.9 %copy-start.7 = (f32[256,128]{1,0:T(8,128)S(1)}, f32[256,128]{1,0:T(8,128)}, u32[]{:S(2)}) copy-start(f32[256,128]{1,0:T(8,128)} %noise_ref.1) | copy-start | bytes 393220
  84.0 39.9 %copy-start.8 = (s32[256]{0:T(256)S(1)}, s32[256]{0:T(256)}, u32[]{:S(2)}) copy-start(s32[256]{0:T(256)} %grid_ref.3) | copy-start | bytes 3076
  84.0 39.9 %copy-start.9 = (s32[256]{0:T(256)S(1)}, s32[256]{0:T(256)}, u32[]{:S(2)}) copy-start(s32[256]{0:T(256)} %counts_ref.3) | copy-start | bytes 3076

commit v5 on v4

--- a/solution.py
+++ b/solution.py
@@ -180,9 +180,8 @@
         plane = jnp.concatenate([wide_y[q : q + 1] * wide_x for q in range(BOX)], 0)
         high, low = split(plane)
         col = column(row, taps_ref)
-        box = mm(
-            jnp.concatenate([high, low, high], 1), jnp.concatenate([col[0], col[0], col[1]], 1), NT
-        )
+        turned = [jnp.transpose(part) for part in col]
+        box = mm(jnp.concatenate([high, low, high], 1), jnp.concatenate([turned[0], turned[0], turned[1]], 0))
         g = grid_ref[t]
         gx = g // GROW
         gy = g - gx * GROW

time: 142 us -> 138 us (0.972)
  Pallas kernels: 52.8 us -> 49.2 us
    pallas_call x1, Pallas kernels: 25.2 us -> 21.7 us  [body(): pl.pallas_call(spread_kernel, out_shape=exchange, in_specs=[smem] * 2 + [...]
where the time goes in v5:
time: 138 us
  Pallas kernels  49.2 us (36%)
  blocking collectives  39.8 us (29%)
  waiting for transfers between devices  34.9 us (25%)
  starting transfers between devices  11.6 us (8%)
  local copies, waits for them, and re-layouts  2.1 us (2%)
    all_to_all x1, blocking collectives, regroup(): lax.all_to_all(array, ('gx', 'gy'), split_axis=0, concat_axis=0, tiled=True)  39.8 us
    all_to_all x1, waiting for transfers between devices, regroup(): lax.all_to_all(array, ('gx', 'gy'), split_axis=0, concat_axis=0, tiled=True)  34.9 us
    pallas_call x1, Pallas kernels, body(): pl.pallas_call(spread_kernel, out_shape=exchange, in_specs=[smem] * 2 + [...  21.7 us
    pallas_call x1, Pallas kernels, body(): pl.pallas_call(sample_kernel, out_shape=jax.ShapeDtypeStruct((tiles, PTS)...  17.3 us
    all_to_all x1, starting transfers between devices, regroup(): lax.all_to_all(array, ('gx', 'gy'), split_axis=0, concat_axis=0, tiled=True)  11.6 us
    pallas_call x1, Pallas kernels, body(): pl.pallas_call(filter_kernel, out_shape=exchange, in_specs=[smem] * 2 + [...  10.3 us
  transfers between devices with their start and end apart: 1, of which 1 were waited for; matrix products, arithmetic and copies ran while one was open for 0% of the time, Pallas kernels for 0%

profile of v5, /device:TPU:1, one launch (start us, length us, event | category | flops | bytes accessed | tf_op | source)
XLA Modules:
  0.0 137.8 jit_solution(7464434622259208511)
XLA Ops:
  0.0 21.7 %shard_map.127 = f32[5120,128]{1,0:T(8,128)} custom-call(s32[256]{0:T(256)} %grid_ref.3, s32[256]{0:T(256)} %counts_ref.3, f32[256,128]{1,0:T(8,128)} %val_ref.3, f32[3,256,128]{2,1,0:T(8,128)} %frac_ref.3, s32[2,256,128]{2,1,0:T(8,128)} %xy_ref.3, s32[256,128]{1,0:T(8,128)} %z_ref.3, bf16[512,256]{1,0:T(8,128)(2,1)} %constant.17.clone.tz_ref), custom_call_target="tpu_custom_call" | custom-call | tf_op jit(solution)/shard_map/pallas_call | solution.py:409
  21.7 0.0 copy-start.12
  21.7 0.0 copy-start.4
  21.7 0.0 copy-start.10
  21.7 0.0 copy-start.11
  21.7 11.6 %all-to-all-start = ((f32[128,40,128]{2,1,0:T(8,128)}), f32[128,40,128]{2,1,0:T(8,128)S(1)}, u32[]{:S(2)}, u32[]{:S(2)}) async-start(f32[128,40,128]{2,1,0:T(8,128)} %bitcast.15), calls=%async_computation | async-start | bytes 5242880 | tf_op jit(solution)/shard_map/all_to_all | solution.py:420
  33.3 0.0 copy-done.12
  33.3 0.1 reshape.25
  33.4 0.1 copy.14
  33.5 34.9 %all-to-all-done = f32[128,40,128]{2,1,0:T(8,128)S(1)} async-done(((f32[128,40,128]{2,1,0:T(8,128)}), f32[128,40,128]{2,1,0:T(8,128)S(1)}, u32[]{:S(2)}, u32[]{:S(2)}) %all-to-all-start) | async-done | bytes 2621472 | tf_op jit(solution)/shard_map/all_to_all | solution.py:420
  68.4 0.0 copy-done.4
  68.4 0.0 copy-done.10
  68.4 0.0 copy-done.11
  68.4 0.0 copy-start
  68.4 1.8 %copy-done = bf16[2,512,1344]{2,1,0:T(8,128)(2,1)S(1)} copy-done((bf16[2,512,1344]{2,1,0:T(8,128)(2,1)S(1)}, bf16[2,512,1344]{2,1,0:T(8,128)(2,1)}, u32[]{:S(2)}) %copy-start) | copy-done | bytes 2752536
  70.2 10.3 %shard_map.128 = f32[5120,128]{1,0:T(8,128)S(1)} custom-call(s32[1]{0:T(128)} %bitcast.dev_ref, f32[256]{0:T(256)S(1)} %copy-done.11, f32[1,512]{1,0:T(1,128)S(1)} %bitcast.13, f32[1,512]{1,0:T(1,128)S(1)} %bitcast.14, f32[5120,128]{1,0:T(8,128)S(1)} %bitcast.11, bf16[2,384,512]{2,1,0:T(8,128)(2,1)S(1)} %copy-done.4, bf16[2,512,1344]{2,1,0:T(8,128)(2,1)S(1)} %copy-done), custom_call_target="tpu_custom_call" | custom-call | tf_op jit(solution)/shard_map/pallas_call | solution.py:427
  80.5 0.0 copy-start.1
  80.5 0.0 copy-start.2
  80.5 0.0 copy-start.3
  80.5 0.0 copy-start.5
  80.6 0.0 copy-start.6
  80.6 0.0 copy-start.7
  80.6 0.0 copy-start.8
  80.6 0.0 copy-start.9
  80.6 39.8 %all_to_all.10 = f32[128,40,128]{2,1,0:T(8,128)S(1)} all-to-all(f32[128,40,128]{2,1,0:T(8,128)S(1)} %bitcast.12), channel_id=1, replica_groups=mesh['gx'=8,'gy'=16] {'gx','gy'}, dimensions={0} | all-to-all | bytes 5242880 | tf_op jit(solution)/shard_map/all_to_all | solution.py:420
  120.4 0.0 copy-done.1
  120.4 0.0 copy-done.2
  120.4 0.0 copy-done.3
  120.4 0.0 copy-done.5
  120.4 0.0 copy-done.6
  120.4 0.0 copy-done.7
  120.4 0.0 copy-done.8
  120.4 0.0 copy-done.9
  120.5 17.3 %shard_map.129 = f32[256,128]{1,0:T(8,128)} custom-call(s32[256]{0:T(256)S(1)} %copy-done.8, s32[256]{0:T(256)S(1)} %copy-done.9, f32[256,128]{1,0:T(8,128)S(1)} %copy-done.5, f32[256,128]{1,0:T(8,128)S(1)} %copy-done.7, f32[3,256,128]{2,1,0:T(8,128)S(1)} %copy-done.1, s32[2,256,128]{2,1,0:T(8,128)S(1)} %copy-done.2, s32[256,128]{1,0:T(8,128)S(1)} %copy-done.6, ...), custom_call_target="tpu_custom_call" | custom-call | tf_op jit(solution)/shard_map/pallas_call | solution.py:447
  (1 shorter events, 0.0 us)
Async XLA Ops:
  21.7 11.6 %copy-start.12 = (f32[512]{0:T(512)S(1)}, f32[512]{0:T(512)}, u32[]{:S(2)}) copy-start(f32[512]{0:T(512)} %param.20) | copy-start | bytes 6148
  21.7 46.7 %copy-start.4 = (bf16[2,384,512]{2,1,0:T(8,128)(2,1)S(1)}, bf16[2,384,512]{2,1,0:T(8,128)(2,1)}, u32[]{:S(2)}) copy-start(bf16[2,384,512]{2,1,0:T(8,128)(2,1)} %constant.18.clone.x_ref) | copy-start | bytes 2359300
  21.7 46.7 %copy-start.10 = (f32[512]{0:T(512)S(1)}, f32[512]{0:T(512)}, u32[]{:S(2)}) copy-start(f32[512]{0:T(512)} %param.21) | copy-start | bytes 6148
  21.7 46.7 %copy-start.11 = (f32[256]{0:T(256)S(1)}, f32[256]{0:T(256)}, u32[]{:S(2)}) copy-start(f32[256]{0:T(256)} %rz_ref.1) | copy-start | bytes 3076
  21.7 46.7 %all-to-all-start = ((f32[128,40,128]{2,1,0:T(8,128)}), f32[128,40,128]{2,1,0:T(8,128)S(1)}, u32[]{:S(2)}, u32[]{:S(2)}) async-start(f32[128,40,128]{2,1,0:T(8,128)} %bitcast.15), calls=%async_computation | async-start | bytes 5242880 | tf_op jit(solution)/shard_map/all_to_all | solution.py:420
  68.4 1.8 %copy-start = (bf16[2,512,1344]{2,1,0:T(8,128)(2,1)S(1)}, bf16[2,512,1344]{2,1,0:T(8,128)(2,1)}, u32[]{:S(2)}) copy-start(bf16[2,512,1344]{2,1,0:T(8,128)(2,1)} %constant.19.clone.ey_ref) | copy-start | bytes 8257540
  80.5 39.9 %copy-start.1 = (f32[3,256,128]{2,1,0:T(8,128)S(1)}, f32[3,256,128]{2,1,0:T(8,128)}, u32[]{:S(2)}) copy-start(f32[3,256,128]{2,1,0:T(8,128)} %frac_ref.3) | copy-start | bytes 1179652
  80.5 39.9 %copy-start.2 = (s32[2,256,128]{2,1,0:T(8,128)S(1)}, s32[2,256,128]{2,1,0:T(8,128)}, u32[]{:S(2)}) copy-start(s32[2,256,128]{2,1,0:T(8,128)} %xy_ref.3) | copy-start | bytes 786436
  80.5 39.9 %copy-start.3 = (bf16[512,256]{1,0:T(8,128)(2,1)S(1)}, bf16[512,256]{1,0:T(8,128)(2,1)}, u32[]{:S(2)}) copy-start(bf16[512,256]{1,0:T(8,128)(2,1)} %constant.17.clone.tz_ref) | copy-start | bytes 786436
  80.5 39.9 %copy-start.5 = (f32[256,128]{1,0:T(8,128)S(1)}, f32[256,128]{1,0:T(8,128)}, u32[]{:S(2)}) copy-start(f32[256,128]{1,0:T(8,128)} %val_ref.3) | copy-start | bytes 393220
  80.6 39.9 %copy-start.6 = (s32[256,128]{1,0:T(8,128)S(1)}, s32[256,128]{1,0:T(8,128)}, u32[]{:S(2)}) copy-start(s32[256,128]{1,0:T(8,128)} %z_ref.3) | copy-start | bytes 393220
  80.6 39.9 %copy-start.7 = (f32[256,128]{1,0:T(8,128)S(1)}, f32[256,128]{1,0:T(8,128)}, u32[]{:S(2)}) copy-start(f32[256,128]{1,0:T(8,128)} %noise_ref.1) | copy-start | bytes 393220
  80.6 39.9 %copy-start.8 = (s32[256]{0:T(256)S(1)}, s32[256]{0:T(256)}, u32[]{:S(2)}) copy-start(s32[256]{0:T(256)} %grid_ref.3) | copy-start | bytes 3076
  80.6 39.9 %copy-start.9 = (s32[256]{0:T(256)S(1)}, s32[256]{0:T(256)}, u32[]{:S(2)}) copy-start(s32[256]{0:T(256)} %counts_ref.3) | copy-start | bytes 3076

commit v6 on v5

--- a/solution.py
+++ b/solution.py
@@ -181,7 +181,7 @@
         high, low = split(plane)
         col = column(row, taps_ref)
         turned = [jnp.transpose(part) for part in col]
-        box = mm(jnp.concatenate([high, low, high], 1), jnp.concatenate([turned[0], turned[0], turned[1]], 0))
+        box = mm(jnp.concatenate([high, low], 1), jnp.concatenate([turned[0], turned[0]], 0)) + mm(high, turned[1])
         g = grid_ref[t]
         gx = g // GROW
         gy = g - gx * GROW
@@ -319,11 +319,11 @@
                     :, 128 * n : 128 * (n + 1)
                 ]
 
-    ends = slice(EX, EX + 24)
+    ends = slice(EX, EX + 32)
     tall = split(
         jnp.concatenate(
             [
-                mm3((x_ref[0, ends, :], x_ref[1, ends, :]), (wh_ref[z], wl_ref[z]), NT)
+                mm3((x_ref[0, ends, :], x_ref[1, ends, :]), (wh_ref[z], wl_ref[z]), NT)[:24]
                 for z in range(2)
             ],
             0,

time: 138 us -> 136 us (0.986)
  Pallas kernels: 49.2 us -> 47.6 us
    pallas_call x1, Pallas kernels: 21.7 us -> 20.1 us  [body(): pl.pallas_call(spread_kernel, out_shape=exchange, in_specs=[smem] * 2 + [...]
where the time goes in v6:
time: 136 us
  Pallas kernels  47.6 us (35%)
  blocking collectives  39.8 us (29%)
  waiting for transfers between devices  34.9 us (26%)
  starting transfers between devices  11.4 us (8%)
  local copies, waits for them, and re-layouts  2.1 us (2%)
    all_to_all x1, blocking collectives, regroup(): lax.all_to_all(array, ('gx', 'gy'), split_axis=0, concat_axis=0, tiled=True)  39.8 us
    all_to_all x1, waiting for transfers between devices, regroup(): lax.all_to_all(array, ('gx', 'gy'), split_axis=0, concat_axis=0, tiled=True)  34.9 us
    pallas_call x1, Pallas kernels, body(): pl.pallas_call(spread_kernel, out_shape=exchange, in_specs=[smem] * 2 + [...  20.1 us
    pallas_call x1, Pallas kernels, body(): pl.pallas_call(sample_kernel, out_shape=jax.ShapeDtypeStruct((tiles, PTS)...  17.3 us
    all_to_all x1, starting transfers between devices, regroup(): lax.all_to_all(array, ('gx', 'gy'), split_axis=0, concat_axis=0, tiled=True)  11.4 us
    pallas_call x1, Pallas kernels, body(): pl.pallas_call(filter_kernel, out_shape=exchange, in_specs=[smem] * 2 + [...  10.2 us
  transfers between devices with their start and end apart: 1, of which 1 were waited for; matrix products, arithmetic and copies ran while one was open for 0% of the time, Pallas kernels for 0%

profile of v6, /device:TPU:1, one launch (start us, length us, event | category | flops | bytes accessed | tf_op | source)
XLA Modules:
  0.0 135.9 jit_solution(17891657515137195648)
XLA Ops:
  0.0 20.1 %shard_map.127 = f32[5120,128]{1,0:T(8,128)} custom-call(s32[256]{0:T(256)} %grid_ref.3, s32[256]{0:T(256)} %counts_ref.3, f32[256,128]{1,0:T(8,128)} %val_ref.3, f32[3,256,128]{2,1,0:T(8,128)} %frac_ref.3, s32[2,256,128]{2,1,0:T(8,128)} %xy_ref.3, s32[256,128]{1,0:T(8,128)} %z_ref.3, bf16[512,256]{1,0:T(8,128)(2,1)} %constant.17.clone.tz_ref), custom_call_target="tpu_custom_call" | custom-call | tf_op jit(solution)/shard_map/pallas_call | solution.py:409
  20.1 0.0 copy-start.12
  20.1 0.0 copy-start.4
  20.1 0.0 copy-start.10
  20.1 0.0 copy-start.11
  20.1 11.4 %all-to-all-start = ((f32[128,40,128]{2,1,0:T(8,128)}), f32[128,40,128]{2,1,0:T(8,128)S(1)}, u32[]{:S(2)}, u32[]{:S(2)}) async-start(f32[128,40,128]{2,1,0:T(8,128)} %bitcast.15), calls=%async_computation | async-start | bytes 5242880 | tf_op jit(solution)/shard_map/all_to_all | solution.py:420
  31.5 0.0 copy-done.12
  31.5 0.1 reshape.25
  31.6 0.1 copy.14
  31.7 34.9 %all-to-all-done = f32[128,40,128]{2,1,0:T(8,128)S(1)} async-done(((f32[128,40,128]{2,1,0:T(8,128)}), f32[128,40,128]{2,1,0:T(8,128)S(1)}, u32[]{:S(2)}, u32[]{:S(2)}) %all-to-all-start) | async-done | bytes 2621472 | tf_op jit(solution)/shard_map/all_to_all | solution.py:420
  66.6 0.0 copy-done.4
  66.6 0.0 copy-done.10
  66.6 0.0 copy-done.11
  66.6 0.0 copy-start
  66.6 1.8 %copy-done = bf16[2,512,1344]{2,1,0:T(8,128)(2,1)S(1)} copy-done((bf16[2,512,1344]{2,1,0:T(8,128)(2,1)S(1)}, bf16[2,512,1344]{2,1,0:T(8,128)(2,1)}, u32[]{:S(2)}) %copy-start) | copy-done | bytes 2752536
  68.4 10.2 %shard_map.128 = f32[5120,128]{1,0:T(8,128)S(1)} custom-call(s32[1]{0:T(128)} %bitcast.dev_ref, f32[256]{0:T(256)S(1)} %copy-done.11, f32[1,512]{1,0:T(1,128)S(1)} %bitcast.13, f32[1,512]{1,0:T(1,128)S(1)} %bitcast.14, f32[5120,128]{1,0:T(8,128)S(1)} %bitcast.11, bf16[2,384,512]{2,1,0:T(8,128)(2,1)S(1)} %copy-done.4, bf16[2,512,1344]{2,1,0:T(8,128)(2,1)S(1)} %copy-done), custom_call_target="tpu_custom_call" | custom-call | tf_op jit(solution)/shard_map/pallas_call | solution.py:427
  78.7 0.0 copy-start.1
  78.7 0.0 copy-start.2
  78.7 0.0 copy-start.3
  78.7 0.0 copy-start.5
  78.7 0.0 copy-start.6
  78.7 0.0 copy-start.7
  78.8 0.0 copy-start.8
  78.8 0.0 copy-start.9
  78.8 39.8 %all_to_all.10 = f32[128,40,128]{2,1,0:T(8,128)S(1)} all-to-all(f32[128,40,128]{2,1,0:T(8,128)S(1)} %bitcast.12), channel_id=1, replica_groups=mesh['gx'=8,'gy'=16] {'gx','gy'}, dimensions={0} | all-to-all | bytes 5242880 | tf_op jit(solution)/shard_map/all_to_all | solution.py:420
  118.6 0.0 copy-done.1
  118.6 0.0 copy-done.2
  118.6 0.0 copy-done.3
  118.6 0.0 copy-done.5
  118.6 0.0 copy-done.6
  118.6 0.0 copy-done.7
  118.6 0.0 copy-done.8
  118.6 0.0 copy-done.9
  118.6 17.3 %shard_map.129 = f32[256,128]{1,0:T(8,128)} custom-call(s32[256]{0:T(256)S(1)} %copy-done.8, s32[256]{0:T(256)S(1)} %copy-done.9, f32[256,128]{1,0:T(8,128)S(1)} %copy-done.5, f32[256,128]{1,0:T(8,128)S(1)} %copy-done.7, f32[3,256,128]{2,1,0:T(8,128)S(1)} %copy-done.1, s32[2,256,128]{2,1,0:T(8,128)S(1)} %copy-done.2, s32[256,128]{1,0:T(8,128)S(1)} %copy-done.6, ...), custom_call_target="tpu_custom_call" | custom-call | tf_op jit(solution)/shard_map/pallas_call | solution.py:447
  (1 shorter events, 0.0 us)
Async XLA Ops:
  20.1 11.4 %copy-start.12 = (f32[512]{0:T(512)S(1)}, f32[512]{0:T(512)}, u32[]{:S(2)}) copy-start(f32[512]{0:T(512)} %param.20) | copy-start | bytes 6148
  20.1 46.5 %copy-start.4 = (bf16[2,384,512]{2,1,0:T(8,128)(2,1)S(1)}, bf16[2,384,512]{2,1,0:T(8,128)(2,1)}, u32[]{:S(2)}) copy-start(bf16[2,384,512]{2,1,0:T(8,128)(2,1)} %constant.18.clone.x_ref) | copy-start | bytes 2359300
  20.1 46.5 %copy-start.10 = (f32[512]{0:T(512)S(1)}, f32[512]{0:T(512)}, u32[]{:S(2)}) copy-start(f32[512]{0:T(512)} %param.21) | copy-start | bytes 6148
  20.1 46.5 %copy-start.11 = (f32[256]{0:T(256)S(1)}, f32[256]{0:T(256)}, u32[]{:S(2)}) copy-start(f32[256]{0:T(256)} %rz_ref.1) | copy-start | bytes 3076
  20.1 46.5 %all-to-all-start = ((f32[128,40,128]{2,1,0:T(8,128)}), f32[128,40,128]{2,1,0:T(8,128)S(1)}, u32[]{:S(2)}, u32[]{:S(2)}) async-start(f32[128,40,128]{2,1,0:T(8,128)} %bitcast.15), calls=%async_computation | async-start | bytes 5242880 | tf_op jit(solution)/shard_map/all_to_all | solution.py:420
  66.6 1.8 %copy-start = (bf16[2,512,1344]{2,1,0:T(8,128)(2,1)S(1)}, bf16[2,512,1344]{2,1,0:T(8,128)(2,1)}, u32[]{:S(2)}) copy-start(bf16[2,512,1344]{2,1,0:T(8,128)(2,1)} %constant.19.clone.ey_ref) | copy-start | bytes 8257540
  78.7 39.9 %copy-start.1 = (f32[3,256,128]{2,1,0:T(8,128)S(1)}, f32[3,256,128]{2,1,0:T(8,128)}, u32[]{:S(2)}) copy-start(f32[3,256,128]{2,1,0:T(8,128)} %frac_ref.3) | copy-start | bytes 1179652
  78.7 39.9 %copy-start.2 = (s32[2,256,128]{2,1,0:T(8,128)S(1)}, s32[2,256,128]{2,1,0:T(8,128)}, u32[]{:S(2)}) copy-start(s32[2,256,128]{2,1,0:T(8,128)} %xy_ref.3) | copy-start | bytes 786436
  78.7 39.9 %copy-start.3 = (bf16[512,256]{1,0:T(8,128)(2,1)S(1)}, bf16[512,256]{1,0:T(8,128)(2,1)}, u32[]{:S(2)}) copy-start(bf16[512,256]{1,0:T(8,128)(2,1)} %constant.17.clone.tz_ref) | copy-start | bytes 786436
  78.7 39.9 %copy-start.5 = (f32[256,128]{1,0:T(8,128)S(1)}, f32[256,128]{1,0:T(8,128)}, u32[]{:S(2)}) copy-start(f32[256,128]{1,0:T(8,128)} %val_ref.3) | copy-start | bytes 393220
  78.7 39.9 %copy-start.6 = (s32[256,128]{1,0:T(8,128)S(1)}, s32[256,128]{1,0:T(8,128)}, u32[]{:S(2)}) copy-start(s32[256,128]{1,0:T(8,128)} %z_ref.3) | copy-start | bytes 393220
  78.7 39.9 %copy-start.7 = (f32[256,128]{1,0:T(8,128)S(1)}, f32[256,128]{1,0:T(8,128)}, u32[]{:S(2)}) copy-start(f32[256,128]{1,0:T(8,128)} %noise_ref.1) | copy-start | bytes 393220
  78.8 39.9 %copy-start.8 = (s32[256]{0:T(256)S(1)}, s32[256]{0:T(256)}, u32[]{:S(2)}) copy-start(s32[256]{0:T(256)} %grid_ref.3) | copy-start | bytes 3076
  78.8 39.9 %copy-start.9 = (s32[256]{0:T(256)S(1)}, s32[256]{0:T(256)}, u32[]{:S(2)}) copy-start(s32[256]{0:T(256)} %counts_ref.3) | copy-start | bytes 3076
